TPU v7x, 128 devices: a whole 4x4x4 slice. The times are simulated.
128 devices in a mesh: section: 8 (over z, core), head: 16 (over x, y).
Axes of the slice: x: 4, y: 4, z: 4, core: 2. Of those that a mesh axis runs over, the one named last changes fastest.
Arguments:
- latents: bfloat16 [4, 256, 3072], P(None, 'head'), may hold values from -6 to 6
- patch_numbers: int32 [3], replicated, may hold values from 0 to 3
- prior_step_cache: bfloat16 [8, 16, 256, 2, 2048], P('section', None, 'head'), may hold values from -6 to 6
- old_block_index: int32 [8, 3, 4], P('section'), may hold values from 0 to 15
- modulation_offset: float32 [8, 3072], P('section'), may hold values from -3 to 3
- modulation_scale: float32 [8, 3072], P('section'), may hold values from -3 to 3
- modulation_gate: float32 [8, 3072], P('section'), may hold values from 0.5 to 1.5
- query_key_value_weight: bfloat16 [8, 3072, 3, 2048], P('section', None, None, 'head'), may hold values from -0.109375 to 0.109375
- feedforward_input_weight: bfloat16 [8, 3072, 12288], P('section', None, 'head'), may hold values from -0.109375 to 0.109375
- adapter_down_weight: bfloat16 [8, 3072, 64], P('section'), may hold values from -0.109375 to 0.109375
- adapter_up_query_key_value: bfloat16 [8, 64, 3, 2048], P('section', None, None, 'head'), may hold values from -0.75 to 0.75
- adapter_up_feedforward: bfloat16 [8, 64, 12288], P('section', None, 'head'), may hold values from -0.75 to 0.75
- attention_output_weight: bfloat16 [8, 2048, 3072], P('section', 'head'), may hold values from -0.5 to 0.5
- feedforward_output_weight: bfloat16 [8, 12288, 3072], P('section', 'head'), may hold values from -0.0546875 to 0.0546875
Outputs:
- hidden: bfloat16 [8, 3, 256, 3072], P('section', None, 'head')
All inputs are finite; a program needn't handle non-finite values.
Results may differ from a plain program's by a relative error of at most 0.033.
Values may be sent and summed in bfloat16 or wider, within the bound.
A program may use at most 128 MiB of HBM per device.

v0:
```python
import math

import jax
import jax.numpy as jnp
from jax import lax
from jax.sharding import PartitionSpec as P

DH = 128
HEADS = 16


def from_behind(value, axis, steps):
    count = lax.axis_size(axis)
    first, last = (max(0, -steps), min(count, count - steps))
    return lax.ppermute(value, axis, [(source, source + steps) for source in range(first, last)])


def modulate(resid, shift, scale):
    values = resid.astype(jnp.float32)
    center = values - jnp.mean(values, axis=-1, keepdims=True)
    spread = jnp.mean(center * center, axis=-1, keepdims=True)
    normed = center * lax.rsqrt(spread + 1e-06)
    return (normed * (1.0 + scale) + shift).astype(jnp.bfloat16)


def rms_unit(values):
    return values * lax.rsqrt(jnp.mean(values * values, axis=-1, keepdims=True) + 1e-06)


def project_rows(piece, w_attn, w_ffn, down_product, adapter_attention_up, adapter_feedforward_up):
    lowrank = jnp.dot(piece, down_product, preferred_element_type=jnp.float32).astype(jnp.bfloat16)
    attn_part = jnp.dot(piece, w_attn, preferred_element_type=jnp.float32)
    attn_part = attn_part + jnp.dot(
        lowrank, adapter_attention_up, preferred_element_type=jnp.float32
    )
    ffn_part = jnp.dot(piece, w_ffn, preferred_element_type=jnp.float32)
    ffn_part = ffn_part + jnp.dot(
        lowrank, adapter_feedforward_up, preferred_element_type=jnp.float32
    )
    return jnp.concatenate([attn_part, ffn_part], axis=1)


def attend(linear, stale, heads_here, head_size):
    rows = linear.shape[0]
    width = 3 * heads_here * head_size
    qkv = linear[:, :width].reshape(rows, 3, heads_here, head_size)
    queries = rms_unit(qkv[:, 0]).astype(jnp.bfloat16)
    keys_new = rms_unit(qkv[:, 1]).astype(jnp.bfloat16)
    values_new = qkv[:, 2].astype(jnp.bfloat16)
    activation = jax.nn.gelu(linear[:, width:], approximate=True).astype(jnp.bfloat16)
    cached_keys = stale[:, :, 0].reshape(-1, heads_here, head_size).astype(jnp.float32)
    cached_keys = rms_unit(cached_keys).astype(jnp.bfloat16)
    cached_values = stale[:, :, 1].reshape(-1, heads_here, head_size)
    all_keys = jnp.concatenate([keys_new, cached_keys], axis=0)
    all_values = jnp.concatenate([values_new, cached_values], axis=0)
    scores = jnp.einsum(
        "qhd,khd->hqk", queries, all_keys, preferred_element_type=jnp.float32
    ) / math.sqrt(head_size)
    expo = jnp.exp(scores)
    weights = (expo / jnp.sum(expo, axis=-1, keepdims=True)).astype(jnp.bfloat16)
    mixed = jnp.einsum("hqk,khd->qhd", weights, all_values, preferred_element_type=jnp.float32)
    return (mixed.astype(jnp.bfloat16).reshape(rows, heads_here * head_size), activation)


def per_device(
    latents,
    patch_numbers,
    prior_step_cache,
    old_block_index,
    modulation_offset,
    modulation_scale,
    modulation_gate,
    query_key_value_weight,
    feedforward_input_weight,
    adapter_down_weight,
    adapter_up_query_key_value,
    adapter_up_feedforward,
    attention_output_weight,
    feedforward_output_weight,
):
    groups = lax.axis_size("head")
    sections = lax.axis_size("section")
    section_index = lax.axis_index("section")
    head_size = DH
    heads_here = HEADS // groups
    tok_dev = latents.shape[1]
    model_dim = latents.shape[2]
    patch_count = old_block_index.shape[1]
    w_attn = query_key_value_weight[0].reshape(model_dim, -1)
    adapter_attention_up = adapter_up_query_key_value[0].reshape(
        adapter_up_query_key_value.shape[1], -1
    )
    w_ffn = feedforward_input_weight[0]
    adapter_feedforward_up = adapter_up_feedforward[0]
    down_product = adapter_down_weight[0]
    out_attn = attention_output_weight[0]
    out_ffn = feedforward_output_weight[0]
    shift = modulation_offset[0]
    scale = modulation_scale[0]
    gate = modulation_gate[0]
    cache = prior_step_cache[0]
    blocks = old_block_index[0]
    attn_cols = 3 * heads_here * head_size
    columns = attn_cols + w_ffn.shape[1]
    total_steps = patch_count + sections - 1

    def stale_for(layer_index):
        chosen = jnp.take(cache, blocks[layer_index], axis=0)
        return lax.all_to_all(chosen, "head", split_axis=3, concat_axis=1, tiled=True)

    def core(linear, stale, active):
        rows = linear.shape[0]

        def core_compute():
            return attend(linear, stale, heads_here, head_size)

        def core_skip():
            return (
                jnp.zeros((rows, heads_here * head_size), jnp.bfloat16),
                jnp.zeros((rows, w_ffn.shape[1]), jnp.bfloat16),
            )

        return lax.cond(active, core_compute, core_skip)

    def out_term(mixed, activation, active):

        def out_compute():
            term = jnp.dot(mixed, out_attn, preferred_element_type=jnp.float32)
            return term + jnp.dot(activation, out_ffn, preferred_element_type=jnp.float32)

        def out_skip():
            return jnp.zeros((mixed.shape[0], model_dim), jnp.float32)

        return lax.cond(active, out_compute, out_skip)

    def locate(step):
        index_raw = step - section_index
        active = jnp.logical_and(index_raw >= 0, index_raw < patch_count)
        return (active, jnp.clip(index_raw, 0, patch_count - 1))

    record_init = jnp.zeros((patch_count, tok_dev, model_dim), jnp.bfloat16)

    def advance_split(step, carry):
        incoming, record = carry
        active, layer_index = locate(step)
        first = lax.dynamic_index_in_dim(latents, patch_numbers[layer_index], 0, keepdims=False)
        resid = jnp.where(section_index == 0, first, incoming)
        modded = modulate(resid, shift, scale)
        piece = lax.all_gather(modded, "head", axis=0, tiled=True)
        linear = lax.cond(
            active,
            lambda: project_rows(
                piece, w_attn, w_ffn, down_product, adapter_attention_up, adapter_feedforward_up
            ),
            lambda: jnp.zeros((piece.shape[0], columns), jnp.float32),
        )
        stale = stale_for(layer_index)
        mixed, activation = core(linear, stale, active)
        summed = lax.psum_scatter(
            out_term(mixed, activation, active).astype(jnp.bfloat16),
            "head",
            scatter_dimension=0,
            tiled=True,
        ).astype(jnp.float32)
        updated = (resid.astype(jnp.float32) + gate * summed).astype(jnp.bfloat16)
        record = jnp.where(
            active, lax.dynamic_update_index_in_dim(record, updated, layer_index, 0), record
        )
        incoming = from_behind(updated, "section", 1)
        return (incoming, record)

    start_rows = jnp.zeros((tok_dev, model_dim), jnp.bfloat16)
    final_in, record = lax.fori_loop(0, total_steps, advance_split, (start_rows, record_init))
    return record[None]


def solution(mesh):
    placed = (
        P(None, "head", None),
        P(),
        P("section", None, "head", None, None),
        P("section", None, None),
        P("section", None),
        P("section", None),
        P("section", None),
        P("section", None, None, "head"),
        P("section", None, "head"),
        P("section", None, None),
        P("section", None, None, "head"),
        P("section", None, "head"),
        P("section", "head", None),
        P("section", "head", None),
    )
    return jax.shard_map(
        per_device,
        mesh=mesh,
        in_specs=placed,
        out_specs=P("section", None, "head", None),
        check_vma=False,
    )
```

profile of v0, /device:TPU:97, one launch (start us, length us, event | category | flops | bytes accessed | tf_op | source)
XLA Modules:
  0.0 1470.8 jit_solution(5310092280443106347)
XLA Ops:
  20.2 1443.7 %while.16 = (s32[]{:T(128)}, bf16[16,3072]{1,0:T(8,128)(2,1)S(1)}, bf16[3,16,3072]{2,1,0:T(8,128)(2,1)}, pred[]{:T(512)}, s32[]{:T(128)}, /*index=5*/s32[3]{0:T(...) while((s32[]{:T(128)}, bf16[16,3072]{1,0:T(8,128)(2,1)S(1)}, ...), condition=%wide.region_14.15_spmd, body=%wide.region_0.14_spmd.sunk | while | flops 3536262400 | bytes 83791328 | solution.py:173
  45.0 10.2 all-to-all-done
  70.5 84.9 %reduce-scatter.2.cloned.1.call-done = bf16[16,3072]{1,0:T(8,128)(2,1)} async-done(((bf16[256,3072]{1,0:T(8,128)(2,1)}), bf16[16,3072]{1,0:T(8,128)(2,1)}) %reduce-scatter.2.cloned.1.call-update) | async-done | bytes 98320 | tf_op jit(solution)/shard_map/while/body/eval_jaxpr/reduce_scatter | solution.py:159
  183.9 9.1 all-to-all-done
  201.7 10.3 all-gather.2.cloned.1.call-done
  213.5 84.9 %reduce-scatter.2.cloned.1.call-done = bf16[16,3072]{1,0:T(8,128)(2,1)} async-done(((bf16[256,3072]{1,0:T(8,128)(2,1)}), bf16[16,3072]{1,0:T(8,128)(2,1)}) %reduce-scatter.2.cloned.1.call-update) | async-done | bytes 98320 | tf_op jit(solution)/shard_map/while/body/eval_jaxpr/reduce_scatter | solution.py:159
  344.7 10.3 all-gather.2.cloned.1.call-done
  356.6 85.9 %reduce-scatter.2.cloned.1.call-done = bf16[16,3072]{1,0:T(8,128)(2,1)} async-done(((bf16[256,3072]{1,0:T(8,128)(2,1)}), bf16[16,3072]{1,0:T(8,128)(2,1)}) %reduce-scatter.2.cloned.1.call-update) | async-done | bytes 98320 | tf_op jit(solution)/shard_map/while/body/eval_jaxpr/reduce_scatter | solution.py:159
  470.9 9.1 all-to-all-done
  488.8 10.3 all-gather.2.cloned.1.call-done
  500.6 85.8 %reduce-scatter.2.cloned.1.call-done = bf16[16,3072]{1,0:T(8,128)(2,1)} async-done(((bf16[256,3072]{1,0:T(8,128)(2,1)}), bf16[16,3072]{1,0:T(8,128)(2,1)}) %reduce-scatter.2.cloned.1.call-update) | async-done | bytes 98320 | tf_op jit(solution)/shard_map/while/body/eval_jaxpr/reduce_scatter | solution.py:159
  614.9 9.1 all-to-all-done
  632.7 10.3 all-gather.2.cloned.1.call-done
  644.5 87.4 %reduce-scatter.2.cloned.1.call-done = bf16[16,3072]{1,0:T(8,128)(2,1)} async-done(((bf16[256,3072]{1,0:T(8,128)(2,1)}), bf16[16,3072]{1,0:T(8,128)(2,1)}) %reduce-scatter.2.cloned.1.call-update) | async-done | bytes 98320 | tf_op jit(solution)/shard_map/while/body/eval_jaxpr/reduce_scatter | solution.py:159
  778.2 10.3 all-gather.2.cloned.1.call-done
  790.1 87.4 %reduce-scatter.2.cloned.1.call-done = bf16[16,3072]{1,0:T(8,128)(2,1)} async-done(((bf16[256,3072]{1,0:T(8,128)(2,1)}), bf16[16,3072]{1,0:T(8,128)(2,1)}) %reduce-scatter.2.cloned.1.call-update) | async-done | bytes 98320 | tf_op jit(solution)/shard_map/while/body/eval_jaxpr/reduce_scatter | solution.py:159
  923.8 10.3 all-gather.2.cloned.1.call-done
  935.7 87.6 %reduce-scatter.2.cloned.1.call-done = bf16[16,3072]{1,0:T(8,128)(2,1)} async-done(((bf16[256,3072]{1,0:T(8,128)(2,1)}), bf16[16,3072]{1,0:T(8,128)(2,1)}) %reduce-scatter.2.cloned.1.call-update) | async-done | bytes 98320 | tf_op jit(solution)/shard_map/while/body/eval_jaxpr/reduce_scatter | solution.py:159
  1069.5 10.3 all-gather.2.cloned.1.call-done
  1096.4 72.2 %reduce-scatter.2.cloned.1.call-done = bf16[16,3072]{1,0:T(8,128)(2,1)} async-done(((bf16[256,3072]{1,0:T(8,128)(2,1)}), bf16[16,3072]{1,0:T(8,128)(2,1)}) %reduce-scatter.2.cloned.1.call-update) | async-done | bytes 98320 | tf_op jit(solution)/shard_map/while/body/eval_jaxpr/reduce_scatter | solution.py:159
  1214.9 10.3 all-gather.2.cloned.1.call-done
  1241.8 72.2 %reduce-scatter.2.cloned.1.call-done = bf16[16,3072]{1,0:T(8,128)(2,1)} async-done(((bf16[256,3072]{1,0:T(8,128)(2,1)}), bf16[16,3072]{1,0:T(8,128)(2,1)}) %reduce-scatter.2.cloned.1.call-update) | async-done | bytes 98320 | tf_op jit(solution)/shard_map/while/body/eval_jaxpr/reduce_scatter | solution.py:159
  1360.3 10.3 all-gather.2.cloned.1.call-done
  1387.2 70.8 %reduce-scatter.2.cloned.1.call-done = bf16[16,3072]{1,0:T(8,128)(2,1)} async-done(((bf16[256,3072]{1,0:T(8,128)(2,1)}), bf16[16,3072]{1,0:T(8,128)(2,1)}) %reduce-scatter.2.cloned.1.call-update) | async-done | bytes 98320 | tf_op jit(solution)/shard_map/while/body/eval_jaxpr/reduce_scatter | solution.py:159
  (519 shorter events, 536.7 us)
Async XLA Ops:
  20.2 48.7 %all-gather.2.cloned.1.call-start = ((), (), s32[]{:S(2)}) async-start(), calls=%async_computation.2 | async-start | bytes 1671168 | tf_op jit(solution)/shard_map/while/body/eval_jaxpr/all_gather | solution.py:149
  38.1 17.1 %all-to-all-start = ((bf16[16,2,8192]{2,1,0:T(2,128)(2,1)}), bf16[16,2,8192]{2,1,0:T(2,128)(2,1)S(1)}, u32[]{:S(2)}, u32[]{:S(2)}) async-start(bf16[16,2,8192]{2,1,0:T(2,128)(2,1)} %reshape.284), calls=%async_computation | async-start | bytes 1048576 | tf_op jit(solution)/shard_map/while/body/eval_jaxpr/all_to_all | solution.py:109
  44.9 110.5 %reduce-scatter.2.cloned.1.call-start = ((), (), s32[]{:S(2)}) async-start(), calls=%async_computation.3 | async-start | bytes 1671168 | tf_op jit(solution)/shard_map/while/body/eval_jaxpr/reduce_scatter | solution.py:159
  161.4 50.6 %all-gather.2.cloned.1.call-start = ((), (), s32[]{:S(2)}) async-start(), calls=%async_computation.2 | async-start | bytes 1671168 | tf_op jit(solution)/shard_map/while/body/eval_jaxpr/all_gather | solution.py:149
  183.8 114.6 %reduce-scatter.2.cloned.1.call-start = ((), (), s32[]{:S(2)}) async-start(), calls=%async_computation.3 | async-start | bytes 1671168 | tf_op jit(solution)/shard_map/while/body/eval_jaxpr/reduce_scatter | solution.py:159
  304.4 50.6 %all-gather.2.cloned.1.call-start = ((), (), s32[]{:S(2)}) async-start(), calls=%async_computation.2 | async-start | bytes 1671168 | tf_op jit(solution)/shard_map/while/body/eval_jaxpr/all_gather | solution.py:149
  326.9 115.6 %reduce-scatter.2.cloned.1.call-start = ((), (), s32[]{:S(2)}) async-start(), calls=%async_computation.3 | async-start | bytes 1671168 | tf_op jit(solution)/shard_map/while/body/eval_jaxpr/reduce_scatter | solution.py:159
  448.4 50.6 %all-gather.2.cloned.1.call-start = ((), (), s32[]{:S(2)}) async-start(), calls=%async_computation.2 | async-start | bytes 1671168 | tf_op jit(solution)/shard_map/while/body/eval_jaxpr/all_gather | solution.py:149
  470.9 115.5 %reduce-scatter.2.cloned.1.call-start = ((), (), s32[]{:S(2)}) async-start(), calls=%async_computation.3 | async-start | bytes 1671168 | tf_op jit(solution)/shard_map/while/body/eval_jaxpr/reduce_scatter | solution.py:159
  592.4 50.6 %all-gather.2.cloned.1.call-start = ((), (), s32[]{:S(2)}) async-start(), calls=%async_computation.2 | async-start | bytes 1671168 | tf_op jit(solution)/shard_map/while/body/eval_jaxpr/all_gather | solution.py:149
  610.2 13.8 all-to-all-start
  614.8 117.1 %reduce-scatter.2.cloned.1.call-start = ((), (), s32[]{:S(2)}) async-start(), calls=%async_computation.3 | async-start | bytes 1671168 | tf_op jit(solution)/shard_map/while/body/eval_jaxpr/reduce_scatter | solution.py:159
  737.9 50.6 %all-gather.2.cloned.1.call-start = ((), (), s32[]{:S(2)}) async-start(), calls=%async_computation.2 | async-start | bytes 1671168 | tf_op jit(solution)/shard_map/while/body/eval_jaxpr/all_gather | solution.py:149
  760.4 117.2 %reduce-scatter.2.cloned.1.call-start = ((), (), s32[]{:S(2)}) async-start(), calls=%async_computation.3 | async-start | bytes 1671168 | tf_op jit(solution)/shard_map/while/body/eval_jaxpr/reduce_scatter | solution.py:159
  883.4 50.7 %all-gather.2.cloned.1.call-start = ((), (), s32[]{:S(2)}) async-start(), calls=%async_computation.2 | async-start | bytes 1671168 | tf_op jit(solution)/shard_map/while/body/eval_jaxpr/all_gather | solution.py:149
  901.3 13.8 all-to-all-start
  905.9 117.3 %reduce-scatter.2.cloned.1.call-start = ((), (), s32[]{:S(2)}) async-start(), calls=%async_computation.3 | async-start | bytes 1671168 | tf_op jit(solution)/shard_map/while/body/eval_jaxpr/reduce_scatter | solution.py:159
  1029.2 50.6 %all-gather.2.cloned.1.call-start = ((), (), s32[]{:S(2)}) async-start(), calls=%async_computation.2 | async-start | bytes 1671168 | tf_op jit(solution)/shard_map/while/body/eval_jaxpr/all_gather | solution.py:149
  1051.7 117.0 %reduce-scatter.2.cloned.1.call-start = ((), (), s32[]{:S(2)}) async-start(), calls=%async_computation.3 | async-start | bytes 1671168 | tf_op jit(solution)/shard_map/while/body/eval_jaxpr/reduce_scatter | solution.py:159
  1174.6 50.6 %all-gather.2.cloned.1.call-start = ((), (), s32[]{:S(2)}) async-start(), calls=%async_computation.2 | async-start | bytes 1671168 | tf_op jit(solution)/shard_map/while/body/eval_jaxpr/all_gather | solution.py:149
  1192.4 13.8 all-to-all-start
  1197.0 117.0 %reduce-scatter.2.cloned.1.call-start = ((), (), s32[]{:S(2)}) async-start(), calls=%async_computation.3 | async-start | bytes 1671168 | tf_op jit(solution)/shard_map/while/body/eval_jaxpr/reduce_scatter | solution.py:159
  1320.0 50.6 %all-gather.2.cloned.1.call-start = ((), (), s32[]{:S(2)}) async-start(), calls=%async_computation.2 | async-start | bytes 1671168 | tf_op jit(solution)/shard_map/while/body/eval_jaxpr/all_gather | solution.py:149
  1342.4 115.6 %reduce-scatter.2.cloned.1.call-start = ((), (), s32[]{:S(2)}) async-start(), calls=%async_computation.3 | async-start | bytes 1671168 | tf_op jit(solution)/shard_map/while/body/eval_jaxpr/reduce_scatter | solution.py:159
  (78 other events, 2040.5 us)
Sparse Core Ops, SparseCore 0:
  24.8 44.1 all-gather.1
  72.2 83.1 reduce-scatter.1
  165.8 46.1 all-gather.1
  215.1 83.3 reduce-scatter.1
  308.9 46.1 all-gather.1
  358.1 84.3 reduce-scatter.1
  452.9 46.1 all-gather.1
  502.3 84.0 reduce-scatter.1
  596.8 46.1 all-gather.1
  646.1 85.8 reduce-scatter.1
  742.4 46.0 all-gather.1
  791.6 85.8 reduce-scatter.1
  887.9 46.1 all-gather.1
  937.2 86.0 reduce-scatter.1
  1033.7 46.0 all-gather.1
  1096.5 72.0 reduce-scatter.1
  1179.1 46.1 all-gather.1
  1241.9 72.0 reduce-scatter.1
  1324.5 46.0 all-gather.1
  1387.4 70.5 reduce-scatter.1
where the time goes:
time: 1480 us; the launch traced here: 1470 us
  waiting for transfers between devices  1050 us (71%)
  local copies, waits for them, and re-layouts  255 us (17%)
  starting transfers between devices  61.6 us (4%)
  matrix products  40.6 us (3%)
  other arithmetic  33.9 us (2%)
  loops' own time  19.9 us (1%)
    reduce_scatter x10, waiting for transfers between devices, advance_split(): lax.psum_scatter(out_term(mixed, activation, active).astype(jnp.bfloat16)...  819 us
    while x120, local copies, waits for them, and re-layouts  117 us
    all_gather x10, waiting for transfers between devices, advance_split(): piece = lax.all_gather(modded, 'head', axis=0, tiled=True)  97.7 us
    all_to_all x10, waiting for transfers between devices, stale_for(): lax.all_to_all(chosen, 'head', split_axis=3, concat_axis=1, tiled=True)  92 us
    all_to_all x10, starting transfers between devices, stale_for(): lax.all_to_all(chosen, 'head', split_axis=3, concat_axis=1, tiled=True)  48.2 us
    select_n x10, local copies, waits for them, and re-layouts, stale_for(): chosen = jnp.take(cache, blocks[layer_index], axis=0)  47 us
    all_to_all x10, local copies, waits for them, and re-layouts, stale_for(): lax.all_to_all(chosen, 'head', split_axis=3, concat_axis=1, tiled=True)  46.1 us
    ppermute x10, waiting for transfers between devices, from_behind(): lax.ppermute(value, axis, [(source, source + steps) for source in range(f...  36.8 us
  transfers between devices with their start and end apart: 40, of which 40 were waited for; matrix products, arithmetic and copies ran while one was open for 15% of the time, Pallas kernels for 0%

commit v1 on v0

v1 whole, which is shorter than its diff:
```python
import math

import jax
import jax.numpy as jnp
from jax import lax
from jax.experimental import pallas as pl
from jax.experimental.pallas import tpu as pltpu
from jax.sharding import PartitionSpec as P

DH = 128
MESH = pl.DeviceIdType.MESH
F32 = jnp.float32
BF16 = jnp.bfloat16
A, B = 0, 1

XP, XM, YP, YM = (1, 0), (-1, 0), (0, 1), (0, -1)
GATHER = [
    (-1, None, None, (0, 0), XP),
    (-1, None, None, (0, 0), XM),
    (-1, None, None, (0, 0), YP),
    (-1, None, None, (0, 0), YM),
    (0, 0, None, XM, XP),
    (0, None, A, XM, YP),
    (0, None, A, XM, YM),
    (1, 1, None, XP, XM),
    (1, None, A, XP, YP),
    (1, None, A, XP, YM),
    (2, 0, None, YM, YP),
    (2, None, B, YM, XP),
    (2, None, B, YM, XM),
    (3, 1, None, YP, YM),
    (3, None, B, YP, XP),
    (3, None, B, YP, XM),
    (4, 0, A, (2, 0), YP),
    (4, 0, A, (2, 0), YM),
    (7, 1, A, (2, 0), YP),
    (7, 1, A, (2, 0), YM),
    (10, 0, B, (0, 2), XP),
    (10, 0, B, (0, 2), XM),
    (13, 1, B, (0, 2), XP),
    (13, 1, B, (0, 2), XM),
    (5, 0, A, (-1, -1), YP),
    (6, 1, A, (-1, 1), YM),
    (8, 0, A, (1, -1), YP),
    (9, 1, A, (1, 1), YM),
    (11, 0, B, (-1, -1), XP),
    (12, 1, B, (1, -1), XM),
    (14, 0, B, (-1, 1), XP),
    (15, 1, B, (1, 1), XM),
    (16, 0, A, (2, -1), YP),
    (19, 1, A, (2, 1), YM),
    (20, 0, B, (-1, 2), XP),
    (23, 1, B, (1, 2), XM),
]
GATHER_WAITS = [0, 1, 2, 3, 4, 7, 10, 13, 5, 6, 8, 9, 11, 12, 14, 15, 16, 19, 20, 23]


def rms_unit(values):
    return values * lax.rsqrt(jnp.mean(values * values, axis=-1, keepdims=True) + 1e-06)


def kernel(
    lat, pn, bidx, off, scl, gate, upq, upf, dnt, cache_hbm, wqkv_hbm, wffn_hbm, woa_hbm, wof_hbm,
    out,
    win, wout, cachev, skv, r1, kv, xin, xg, act, part, rb, tb, r2,
    ag_s, ag_r, rs_s, rs_r, st_s, st_r, x_s, x_r, w_sem,
):
    patches = xin.shape[0]
    sections = lax.axis_size("section")
    sec = lax.axis_index("section")
    head = lax.axis_index("head")
    x = head // 4
    y = lax.rem(head, 4)

    def px(d):
        return lax.rem(x + (d + 4), 4)

    def py(d):
        return lax.rem(y + (d + 4), 4)

    def dev(d):
        return (sec, px(d[0]) * 4 + py(d[1]))

    first_section = sec == 0
    last_section = sec == sections - 1

    w_copies = [
        pltpu.make_async_copy(cache_hbm, cachev, w_sem.at[0]),
        pltpu.make_async_copy(wqkv_hbm.at[0], win.at[:, pl.ds(0, DH)], w_sem.at[1]),
        pltpu.make_async_copy(wqkv_hbm.at[1], win.at[:, pl.ds(DH, DH)], w_sem.at[2]),
        pltpu.make_async_copy(wqkv_hbm.at[2], win.at[:, pl.ds(2 * DH, DH)], w_sem.at[3]),
        pltpu.make_async_copy(wffn_hbm, win.at[:, pl.ds(3 * DH, 768)], w_sem.at[4]),
        pltpu.make_async_copy(woa_hbm, wout.at[pl.ds(0, DH)], w_sem.at[5]),
        pltpu.make_async_copy(wof_hbm, wout.at[pl.ds(DH, 768)], w_sem.at[6]),
    ]
    for copy in w_copies:
        copy.start()

    barrier = pltpu.get_barrier_semaphore()
    for d in (XP, XM, (2, 0), YP, YM, (0, 2)):
        pl.semaphore_signal(barrier, inc=1, device_id=dev(d), device_id_type=MESH)

    for step in (1, sections - 1):
        neighbour = (lax.rem(sec + step, sections), head)
        pl.semaphore_signal(barrier, inc=1, device_id=neighbour, device_id_type=MESH)
    pl.semaphore_wait(barrier, 8)

    def remote(src, dst, ssem, rsem, device):
        return pltpu.make_async_remote_copy(
            src_ref=src, dst_ref=dst, send_sem=ssem, recv_sem=rsem, device_id=device,
            device_id_type=MESH,
        )

    def xg_at(m, q, hf, place):
        qi = slice(None) if q is None else q
        hi = slice(None) if hf is None else hf
        return xg.at[m, qi, hi, px(place[0]), py(place[1])]

    def gather_copy(m, i):
        _, q, hf, place, way = GATHER[i]
        ref = xg_at(m, q, hf, place)
        return remote(ref, ref, ag_s.at[m, i], ag_r.at[m, i], dev(way))

    def gather_landed(m, i):
        _, q, hf, place, way = GATHER[i]
        ref = xg_at(m, q, hf, (place[0] - way[0], place[1] - way[1]))
        remote(ref, ref, ag_s.at[m, i], ag_r.at[m, i], dev((-way[0], -way[1]))).wait_recv()

    def stale_first(m, i):
        if i < 3:
            d = (1, -1, 2)[i]
            return remote(
                skv.at[m, 0, px(d)], r1.at[m, 0, x], st_s.at[m, i], st_r.at[m, i], dev((d, 0))
            )
        d = (1, -1, 2)[i - 3]
        return remote(
            skv.at[m, 1, py(d)], r1.at[m, 1, y], st_s.at[m, i], st_r.at[m, i], dev((0, d))
        )

    def stale_first_landed(m, i):
        if i < 3:
            d = (-1, 1, 2)[i]
            ref, device = r1.at[m, 0, px(d)], dev((d, 0))
        else:
            d = (-1, 1, 2)[i - 3]
            ref, device = r1.at[m, 1, py(d)], dev((0, d))
        remote(ref, ref, st_s.at[m, i], st_r.at[m, i], device).wait_recv()

    def stale_second(m, i):
        if i < 9:
            d = (1, -1, 2)[i - 6]
            return remote(
                r1.at[m, 0, :, py(d)], kv.at[m, 0, y], st_s.at[m, i], st_r.at[m, i], dev((0, d))
            )
        d = (1, -1, 2)[i - 9]
        return remote(
            r1.at[m, 1, :, px(d)], kv.at[m, 1, x], st_s.at[m, i], st_r.at[m, i], dev((d, 0))
        )

    def stale_second_landed(m, i):
        if i < 9:
            d = (-1, 1, 2)[i - 6]
            ref, device = kv.at[m, 0, py(d)], dev((0, d))
        else:
            d = (-1, 1, 2)[i - 9]
            ref, device = kv.at[m, 1, px(d)], dev((d, 0))
        remote(ref, ref, st_s.at[m, i], st_r.at[m, i], device).wait_recv()

    def stale_send(m):
        def one(j, _):
            block = bidx[m, j]
            keys = cachev[0, block].astype(F32)
            values = cachev[1, block]
            rows = pl.ds(pl.multiple_of(j * 16, 16), 16)
            for h in range(16):
                part_k = keys[:, h * DH:(h + 1) * DH]
                skv[m, 0, h // 4, h % 4, rows, :] = rms_unit(part_k).astype(BF16)
                skv[m, 1, h % 4, h // 4, rows, :] = values[:, h * DH:(h + 1) * DH]
            return 0

        lax.fori_loop(0, 4, one, 0)
        for i in range(6):
            stale_first(m, i).start()
        r1[m, 0, x] = skv[m, 0, x]
        r1[m, 1, y] = skv[m, 1, y]

    def stale_forward(m):
        for i in range(3):
            stale_first_landed(m, i)
        for i in range(6, 9):
            stale_second(m, i).start()
        for i in range(3, 6):
            stale_first_landed(m, i)
        for i in range(9, 12):
            stale_second(m, i).start()
        kv[m, 0, y] = r1[m, 0, :, y]
        kv[m, 1, x] = r1[m, 1, :, x]

    ALL = slice(None)
    SUM1 = [
        (lambda m: part.at[m, 0, A, :, py(2)], YM),
        (lambda m: part.at[m, 0, A, :, py(1)], YP),
        (lambda m: part.at[m, 0, B, px(2)], XM),
        (lambda m: part.at[m, 0, B, px(1)], XP),
        (lambda m: part.at[m, 1, A, :, py(2)], YP),
        (lambda m: part.at[m, 1, A, :, py(-1)], YM),
        (lambda m: part.at[m, 1, B, px(2)], XP),
        (lambda m: part.at[m, 1, B, px(-1)], XM),
        (lambda m: part.at[m, 0, A, :, py(-1)], YM),
        (lambda m: part.at[m, 0, B, px(-1)], XM),
        (lambda m: part.at[m, 1, A, :, py(1)], YP),
        (lambda m: part.at[m, 1, B, px(1)], XP),
    ]
    SUM2 = [
        (lambda m: tb.at[m, 0, A, px(2)], XM),
        (lambda m: tb.at[m, 0, A, px(1)], XP),
        (lambda m: tb.at[m, 0, B, py(2)], YM),
        (lambda m: tb.at[m, 0, B, py(1)], YP),
        (lambda m: tb.at[m, 1, A, px(2)], XP),
        (lambda m: tb.at[m, 1, A, px(-1)], XM),
        (lambda m: tb.at[m, 1, B, py(2)], YP),
        (lambda m: tb.at[m, 1, B, py(-1)], YM),
        (lambda m: tb.at[m, 0, A, px(-1)], XM),
        (lambda m: tb.at[m, 0, B, py(-1)], YM),
        (lambda m: tb.at[m, 1, A, px(1)], XP),
        (lambda m: tb.at[m, 1, B, py(1)], YP),
    ]

    def sum_copy(m, i):
        source, way = SUM1[i] if i < 12 else SUM2[i - 12]
        target = rb.at[m, i] if i < 12 else r2.at[m, i - 12]
        return remote(source(m), target, rs_s.at[m, i], rs_r.at[m, i], dev(way))

    def sum_landed(m, i):
        way = SUM1[i][1] if i < 12 else SUM2[i - 12][1]
        target = rb.at[m, i] if i < 12 else r2.at[m, i - 12]
        remote(
            target, target, rs_s.at[m, i], rs_r.at[m, i], dev((-way[0], -way[1]))
        ).wait_recv()

    def hand_on(m):
        return remote(out.at[m], xin.at[m], x_s.at[m], x_r.at[m], (sec + 1, head))

    def modulate_and_send(m):
        @pl.when(first_section)
        def _():
            xin[m] = lat[pn[m]]

        @pl.when(sec > 0)
        def _():
            remote(xin.at[m], xin.at[m], x_s.at[m], x_r.at[m], (sec - 1, head)).wait_recv()

        values = xin[m].astype(F32)
        center = values - jnp.mean(values, axis=-1, keepdims=True)
        spread = jnp.mean(center * center, axis=-1, keepdims=True)
        normed = center * lax.rsqrt(spread + 1e-06)
        modded = (normed * (1.0 + scl[...]) + off[...]).astype(BF16)
        for q in range(2):
            for hf in range(2):
                c = q * 2 + hf
                xg[m, q, hf, x, y] = modded[:, c * 768:(c + 1) * 768]
        for i in range(4):
            gather_copy(m, i).start()

    def gather_rest(m):
        for w in GATHER_WAITS:
            gather_landed(m, w)
            for i, entry in enumerate(GATHER):
                if entry[0] == w:
                    gather_copy(m, i).start()
        for i in range(len(GATHER)):
            if i not in GATHER_WAITS:
                gather_landed(m, i)

    def tokens(m, c):
        return xg[m, c // 2, c % 2].reshape(256, 768)

    def dot(a, b):
        return jnp.dot(a, b, preferred_element_type=F32)

    def dot_nt(a, b):
        return lax.dot_general(a, b, (((1,), (1,)), ((), ())), preferred_element_type=F32)

    def project(m):
        low = dot_nt(tokens(m, 0), dnt[:, 0:768])
        for c in range(1, 4):
            low += dot_nt(tokens(m, c), dnt[:, c * 768:(c + 1) * 768])
        low = low.astype(BF16)
        qkv = []
        for n in range(3):
            acc = dot(low, upq[n])
            for c in range(4):
                acc += dot(tokens(m, c), win[c * 768:(c + 1) * 768, n * DH:(n + 1) * DH])
            qkv.append(acc)

        def feed(n, _):
            cols = pl.ds(pl.multiple_of(n * 256, 256), 256)
            wcols = pl.ds(pl.multiple_of(n * 256 + 3 * DH, DH), 256)
            acols = pl.ds(pl.multiple_of(n * 256 + DH, DH), 256)
            acc = dot(low, upf[:, cols])
            for c in range(4):
                acc += dot(tokens(m, c), win[c * 768:(c + 1) * 768, wcols])
            act[:, acols] = jax.nn.gelu(acc, approximate=True).astype(BF16)
            return 0

        lax.fori_loop(0, 3, feed, 0)
        return qkv

    def attend(m, qkv):
        queries = rms_unit(qkv[0]).astype(BF16)
        fresh_keys = rms_unit(qkv[1]).astype(BF16)
        fresh_values = qkv[2].astype(BF16)
        for i in range(6, 12):
            stale_second_landed(m, i)
        total = jnp.zeros((256, 1), F32)
        mixed = jnp.zeros((256, DH), F32)
        for j in range(5):
            if j == 4:
                keys, values = fresh_keys, fresh_values
            else:
                keys = kv[m, 0, j].reshape(256, DH)
                values = kv[m, 1, :, j].reshape(256, DH)
            expo = jnp.exp(dot_nt(queries, keys) * (1.0 / math.sqrt(DH)))
            total += jnp.sum(expo, axis=-1, keepdims=True)
            mixed += dot(expo.astype(BF16), values)
        act[:, 0:DH] = (mixed / total).astype(BF16)

    def output_products(m):
        for q in range(2):
            for hf in range(2):
                c = q * 2 + hf
                for n in range(3):
                    lo = c * 768 + n * 256
                    term = dot(act[...], wout[:, lo:lo + 256]).astype(BF16)
                    part[m, q, hf, :, :, :, n * 256:(n + 1) * 256] = term.reshape(4, 4, 16, 256)
                sum_copy(m, 2 * c).start()
                sum_copy(m, 2 * c + 1).start()

    def wide(value):
        return value.astype(F32)

    def sum_up(m):
        sum_landed(m, 0)
        part[m, 0, A, :, py(-1)] = (wide(part[m, 0, A, :, py(-1)]) + wide(rb[m, 0])).astype(BF16)
        sum_copy(m, 8).start()
        sum_landed(m, 2)
        part[m, 0, B, px(-1)] = (wide(part[m, 0, B, px(-1)]) + wide(rb[m, 2])).astype(BF16)
        sum_copy(m, 9).start()
        sum_landed(m, 4)
        part[m, 1, A, :, py(1)] = (wide(part[m, 1, A, :, py(1)]) + wide(rb[m, 4])).astype(BF16)
        sum_copy(m, 10).start()
        sum_landed(m, 6)
        part[m, 1, B, px(1)] = (wide(part[m, 1, B, px(1)]) + wide(rb[m, 6])).astype(BF16)
        sum_copy(m, 11).start()
        for q, hf, near, far, a, b in (
            (0, A, 1, 8, 12, 13), (0, B, 3, 9, 14, 15), (1, A, 5, 10, 16, 17), (1, B, 7, 11, 18, 19)
        ):
            sum_landed(m, near)
            sum_landed(m, far)
            mine = part[m, q, hf, :, y] if hf == A else part[m, q, hf, x]
            tb[m, q, hf] = (wide(mine) + wide(rb[m, near]) + wide(rb[m, far])).astype(BF16)
            sum_copy(m, a).start()
            sum_copy(m, b).start()
        for q, hf, came, i in ((0, A, 12, 20), (0, B, 14, 21), (1, A, 16, 22), (1, B, 18, 23)):
            step = -1 if q == 0 else 1
            place = px(step) if hf == A else py(step)
            sum_landed(m, came)
            tb[m, q, hf, place] = (wide(tb[m, q, hf, place]) + wide(r2[m, came - 12])).astype(BF16)
            sum_copy(m, i).start()
        for q, hf, near, far, n1, n2 in (
            (0, A, 1, 8, 13, 20), (0, B, 3, 9, 15, 21), (1, A, 5, 10, 17, 22), (1, B, 7, 11, 19, 23)
        ):
            sum_landed(m, n1)
            sum_landed(m, n2)
            along = x if hf == A else y
            branch = wide(part[m, q, hf, x, y]) + wide(rb[m, near, along]) + wide(rb[m, far, along])
            branch += wide(r2[m, n1 - 12]) + wide(r2[m, n2 - 12])
            c = q * 2 + hf
            cols = slice(c * 768, (c + 1) * 768)
            out[m, :, cols] = (wide(xin[m, :, cols]) + gate[:, cols] * branch).astype(BF16)

        @pl.when(sec < sections - 1)
        def _():
            hand_on(m).start()

    w_copies[0].wait()
    stale_send(0)

    def patch(m, _):
        modulate_and_send(m)

        @pl.when(m == 0)
        def _():
            stale_forward(0)

        gather_rest(m)

        @pl.when(m == 0)
        def _():
            for copy in w_copies[1:]:
                copy.wait()

        @pl.when(m < patches - 1)
        def _():
            stale_send(m + 1)

        attend(m, project(m))
        output_products(m)

        @pl.when(m < patches - 1)
        def _():
            stale_forward(m + 1)

        sum_up(m)
        return 0

    lax.fori_loop(0, patches, patch, 0)

    def drain(m, _):
        for i in range(len(GATHER)):
            gather_copy(m, i).wait_send()
        for i in range(24):
            sum_copy(m, i).wait_send()
        for i in range(6):
            stale_first(m, i).wait_send()
        for i in range(6, 12):
            stale_second(m, i).wait_send()

        @pl.when(sec < sections - 1)
        def _():
            hand_on(m).wait_send()

        return 0

    lax.fori_loop(0, patches, drain, 0)


def per_device(
    latents, patch_numbers, prior_step_cache, old_block_index, modulation_offset, modulation_scale,
    modulation_gate, query_key_value_weight, feedforward_input_weight, adapter_down_weight,
    adapter_up_query_key_value, adapter_up_feedforward, attention_output_weight,
    feedforward_output_weight,
):
    patches = old_block_index.shape[1]
    vmem = pl.BlockSpec(memory_space=pltpu.VMEM)
    smem = pl.BlockSpec(memory_space=pltpu.SMEM)
    hbm = pl.BlockSpec(memory_space=pl.ANY)
    dma = pltpu.SemaphoreType.DMA
    record = pl.pallas_call(
        kernel,
        out_shape=jax.ShapeDtypeStruct((patches, 16, 3072), BF16),
        in_specs=[vmem, smem, smem] + [vmem] * 6 + [hbm] * 5,
        out_specs=vmem,
        scratch_shapes=[
            pltpu.VMEM((3072, 1152), BF16),
            pltpu.VMEM((896, 3072), BF16),
            pltpu.VMEM((2, 16, 16, 2048), BF16),
            pltpu.VMEM((patches, 2, 4, 4, 64, DH), BF16),
            pltpu.VMEM((patches, 2, 4, 4, 64, DH), BF16),
            pltpu.VMEM((patches, 2, 4, 4, 64, DH), BF16),
            pltpu.VMEM((patches, 16, 3072), BF16),
            pltpu.VMEM((patches, 2, 2, 4, 4, 16, 768), BF16),
            pltpu.VMEM((256, 896), BF16),
            pltpu.VMEM((patches, 2, 2, 4, 4, 16, 768), BF16),
            pltpu.VMEM((patches, 12, 4, 16, 768), BF16),
            pltpu.VMEM((patches, 2, 2, 4, 16, 768), BF16),
            pltpu.VMEM((patches, 12, 16, 768), BF16),
            dma((patches, 36)),
            dma((patches, 36)),
            dma((patches, 24)),
            dma((patches, 24)),
            dma((patches, 12)),
            dma((patches, 12)),
            dma((patches,)),
            dma((patches,)),
            dma((7,)),
        ],
        compiler_params=pltpu.CompilerParams(
            collective_id=0, has_side_effects=True, vmem_limit_bytes=58 * 2**20
        ),
        cost_estimate=pl.CostEstimate(
            flops=10_000_000_000, bytes_accessed=16_000_000, transcendentals=2_000_000
        ),
    )(
        latents,
        patch_numbers,
        old_block_index[0],
        modulation_offset,
        modulation_scale,
        modulation_gate,
        adapter_up_query_key_value[0].transpose(1, 0, 2),
        adapter_up_feedforward[0],
        adapter_down_weight[0].T,
        prior_step_cache[0].transpose(2, 0, 1, 3),
        query_key_value_weight[0].transpose(1, 0, 2),
        feedforward_input_weight[0],
        attention_output_weight[0],
        feedforward_output_weight[0],
    )
    return record[None]


def solution(mesh):
    placed = (
        P(None, "head", None),
        P(),
        P("section", None, "head", None, None),
        P("section", None, None),
        P("section", None),
        P("section", None),
        P("section", None),
        P("section", None, None, "head"),
        P("section", None, "head"),
        P("section", None, None),
        P("section", None, None, "head"),
        P("section", None, "head"),
        P("section", "head", None),
        P("section", "head", None),
    )
    return jax.shard_map(
        per_device,
        mesh=mesh,
        in_specs=placed,
        out_specs=P("section", None, "head", None),
        check_vma=False,
    )
```

time: 1480 us -> 412 us (0.28)
  waiting for transfers between devices: 1050 us -> 0 us
  Pallas kernels: 0 us -> 405 us
  local copies, waits for them, and re-layouts: 255 us -> 6.77 us
  starting transfers between devices: 61.6 us -> 0 us
  matrix products: 40.6 us -> 0 us
  other arithmetic: 33.9 us -> 0 us
  loops' own time: 19.9 us -> 0 us
    reduce_scatter x10 -> x0, waiting for transfers between devices: 819 us -> none  [advance_split(): lax.psum_scatter(out_term(mixed, activation, active).astype(jnp.bfloat16)...]
    pallas_call x0 -> x1, Pallas kernels: none -> 405 us  [per_device(): pl.pallas_call(kernel, out_shape=jax.ShapeDtypeStruct((patches, 16, 3072)...]
    while x121 -> x0, local copies, waits for them, and re-layouts: 119 us -> none
    all_gather x10 -> x0, waiting for transfers between devices: 97.7 us -> none  [advance_split(): piece = lax.all_gather(modded, 'head', axis=0, tiled=True)]
    all_to_all x10 -> x0, waiting for transfers between devices: 92 us -> none  [stale_for(): lax.all_to_all(chosen, 'head', split_axis=3, concat_axis=1, tiled=True)]
    all_to_all x10 -> x0, starting transfers between devices: 48.2 us -> none  [stale_for(): lax.all_to_all(chosen, 'head', split_axis=3, concat_axis=1, tiled=True)]
    select_n x10 -> x0, local copies, waits for them, and re-layouts: 47 us -> none  [stale_for(): chosen = jnp.take(cache, blocks[layer_index], axis=0)]
    all_to_all x10 -> x0, local copies, waits for them, and re-layouts: 46.1 us -> none  [stale_for(): lax.all_to_all(chosen, 'head', split_axis=3, concat_axis=1, tiled=True)]
  transfers between devices with their start and end apart: 40 -> 0, of which waited for: 40 -> 0; matrix products, arithmetic and copies ran while one was open for 15% -> 0% of each run, Pallas kernels for 0% -> 0%
where the time goes in v1:
time: 412 us; the launch traced here: 411 us
  Pallas kernels  405 us (98%)
  local copies, waits for them, and re-layouts  6.77 us (2%)
    pallas_call x1, Pallas kernels, per_device(): pl.pallas_call(kernel, out_shape=jax.ShapeDtypeStruct((patches, 16, 3072)...  405 us

profile of v1, /device:TPU:97, one launch (start us, length us, event | category | flops | bytes accessed | tf_op | source)
XLA Modules:
  0.0 411.3 jit_solution(16446188052656991915)
XLA Ops:
  0.0 1.3 copy.20
  1.3 3.8 copy.19
  5.1 404.5 %shard_map.136 = bf16[3,16,3072]{2,1,0:T(8,128)(2,1)} custom-call(bf16[4,16,3072]{2,1,0:T(8,128)(2,1)} %lat.1, s32[3]{0:T(128)} %pn.1, s32[3,4]{1,0:T(4,128)} %bitcast.24, f32[1,3072]{1,0:T(1,128)} %off.1, f32[1,3072]{1,0:T(1,128)} %scl.1, f32[1,3072]{1,0:T(1,128)} %gate.1, bf16[3,64,128]{2,1,0:T(8,128)(2,1)} %bitcast.31, bf16[64,768]{1,0:T(8,128)(2,1)} %bitcast.30, ...), custom_call_target="tpu_custom_call" | custom-call | flops 10000000000 | bytes 16000000 | tf_op jit(solution)/shard_map/pallas_call | solution.py:449
  409.6 1.7 copy.22

commit v2 on v1

v2 whole, which is shorter than its diff:
```python
import math

import jax
import jax.numpy as jnp
from jax import lax
from jax.experimental import pallas as pl
from jax.experimental.pallas import tpu as pltpu
from jax.sharding import PartitionSpec as P

DH = 128
MESH = pl.DeviceIdType.MESH
F32 = jnp.float32
BF16 = jnp.bfloat16
A, B = 0, 1

ORDER = [
    (0, 0), (1, 0), (3, 0), (2, 0), (0, 1), (0, 3), (0, 2),
    (1, 1), (1, 3), (3, 1), (3, 3), (1, 2), (3, 2), (2, 1), (2, 3), (2, 2),
]
EARLY = 7 * 16
FAR_FIRST = (2, 1, 3)
NEAR_FIRST = (1, 3, 2)


def along(axis, d):
    return (d, 0) if axis == 0 else (0, d)


def slot(place):
    return ORDER.index((place[0] % 4, place[1] % 4))


GATHER = []
for axis in (0, 1):
    GATHER += [(axis, (0, 0), along(axis, d)) for d in FAR_FIRST]
for axis in (0, 1):
    GATHER += [(1 - axis, (0, 0), along(axis, d)) for d in FAR_FIRST]
FORWARD = []
for d in NEAR_FIRST:
    for axis in (0, 1):
        first = GATHER.index((axis, (0, 0), along(axis, d)))
        after = [(axis, along(axis, -d % 4), along(1 - axis, e)) for e in FAR_FIRST]
        FORWARD.append((first, range(len(GATHER), len(GATHER) + 3)))
        GATHER += after


def rms_unit(values):
    return values * lax.rsqrt(jnp.mean(values * values, axis=-1, keepdims=True) + 1e-06)


def kernel(
    lat, pn, bidx, off, scl, gate, upq, upf, dnt, cache_hbm, wqkv_hbm, wffn_hbm, woa_hbm, wof_hbm,
    out,
    win, wout, cachev, skv, r1, kv, xin, xg, qkv, act, part, rb, tb, r2,
    ag_s, ag_r, rs_s, rs_r, st_s, st_r, x_s, x_r, w_sem,
):
    patches = xin.shape[0]
    sections = lax.axis_size("section")
    sec = lax.axis_index("section")
    head = lax.axis_index("head")
    x = head // 4
    y = lax.rem(head, 4)

    def px(d):
        return lax.rem(x + (d + 4), 4)

    def py(d):
        return lax.rem(y + (d + 4), 4)

    def dev(d):
        return (sec, px(d[0]) * 4 + py(d[1]))

    first_section = sec == 0
    last_section = sec == sections - 1

    w_copies = [
        pltpu.make_async_copy(cache_hbm, cachev, w_sem.at[0]),
        pltpu.make_async_copy(wqkv_hbm.at[0], win.at[:, pl.ds(0, DH)], w_sem.at[1]),
        pltpu.make_async_copy(wqkv_hbm.at[1], win.at[:, pl.ds(DH, DH)], w_sem.at[2]),
        pltpu.make_async_copy(wqkv_hbm.at[2], win.at[:, pl.ds(2 * DH, DH)], w_sem.at[3]),
        pltpu.make_async_copy(wffn_hbm, win.at[:, pl.ds(3 * DH, 768)], w_sem.at[4]),
        pltpu.make_async_copy(woa_hbm, wout.at[pl.ds(0, DH)], w_sem.at[5]),
        pltpu.make_async_copy(wof_hbm, wout.at[pl.ds(DH, 768)], w_sem.at[6]),
    ]
    for copy in w_copies:
        copy.start()

    barrier = pltpu.get_barrier_semaphore()
    for d in FAR_FIRST:
        for axis in (0, 1):
            pl.semaphore_signal(
                barrier, inc=1, device_id=dev(along(axis, d)), device_id_type=MESH
            )
    for step in (1, sections - 1):
        neighbour = (lax.rem(sec + step, sections), head)
        pl.semaphore_signal(barrier, inc=1, device_id=neighbour, device_id_type=MESH)
    pl.semaphore_wait(barrier, 8)

    def remote(src, dst, ssem, rsem, device):
        return pltpu.make_async_remote_copy(
            src_ref=src, dst_ref=dst, send_sem=ssem, recv_sem=rsem, device_id=device,
            device_id_type=MESH,
        )

    def gather_copy(m, i):
        hf, place, way = GATHER[i]
        there = slot((place[0] - way[0], place[1] - way[1]))
        return remote(
            xg.at[m, hf, slot(place)], xg.at[m, hf, there], ag_s.at[m, i], ag_r.at[m, i], dev(way)
        )

    def gather_landed(m, i):
        hf, place, way = GATHER[i]
        ref = xg.at[m, hf, slot((place[0] - way[0], place[1] - way[1]))]
        remote(ref, ref, ag_s.at[m, i], ag_r.at[m, i], dev((-way[0], -way[1]))).wait_recv()

    def stale_first(m, i):
        if i < 3:
            d = (1, -1, 2)[i]
            return remote(
                skv.at[m, 0, px(d)], r1.at[m, 0, x], st_s.at[m, i], st_r.at[m, i], dev((d, 0))
            )
        d = (1, -1, 2)[i - 3]
        return remote(
            skv.at[m, 1, py(d)], r1.at[m, 1, y], st_s.at[m, i], st_r.at[m, i], dev((0, d))
        )

    def stale_first_landed(m, i):
        if i < 3:
            d = (-1, 1, 2)[i]
            ref, device = r1.at[m, 0, px(d)], dev((d, 0))
        else:
            d = (-1, 1, 2)[i - 3]
            ref, device = r1.at[m, 1, py(d)], dev((0, d))
        remote(ref, ref, st_s.at[m, i], st_r.at[m, i], device).wait_recv()

    def stale_second(m, i):
        if i < 9:
            d = (1, -1, 2)[i - 6]
            return remote(
                r1.at[m, 0, :, py(d)], kv.at[m, 0, y], st_s.at[m, i], st_r.at[m, i], dev((0, d))
            )
        d = (1, -1, 2)[i - 9]
        return remote(
            r1.at[m, 1, :, px(d)], kv.at[m, 1, x], st_s.at[m, i], st_r.at[m, i], dev((d, 0))
        )

    def stale_second_landed(m, i):
        if i < 9:
            d = (-1, 1, 2)[i - 6]
            ref, device = kv.at[m, 0, py(d)], dev((0, d))
        else:
            d = (-1, 1, 2)[i - 9]
            ref, device = kv.at[m, 1, px(d)], dev((d, 0))
        remote(ref, ref, st_s.at[m, i], st_r.at[m, i], device).wait_recv()

    def stale_send(m):
        def one(j, _):
            block = bidx[m, j]
            keys = cachev[0, block].astype(F32)
            values = cachev[1, block]
            rows = pl.ds(pl.multiple_of(j * 16, 16), 16)
            for h in range(16):
                part_k = keys[:, h * DH:(h + 1) * DH]
                skv[m, 0, h // 4, h % 4, rows, :] = rms_unit(part_k).astype(BF16)
                skv[m, 1, h % 4, h // 4, rows, :] = values[:, h * DH:(h + 1) * DH]
            return 0

        lax.fori_loop(0, 4, one, 0)
        for i in range(6):
            stale_first(m, i).start()
        r1[m, 0, x] = skv[m, 0, x]
        r1[m, 1, y] = skv[m, 1, y]

    def stale_forward(m):
        for i in range(3):
            stale_first_landed(m, i)
        for i in range(6, 9):
            stale_second(m, i).start()
        for i in range(3, 6):
            stale_first_landed(m, i)
        for i in range(9, 12):
            stale_second(m, i).start()
        kv[m, 0, y] = r1[m, 0, :, y]
        kv[m, 1, x] = r1[m, 1, :, x]

    def sum_way(i):
        second, c, d = i // 12, i % 12 // 3, FAR_FIRST[i % 3]
        return c, d, along((1 - c % 2) if second == 0 else c % 2, d)

    def sum_copy(m, i):
        c, d, way = sum_way(i)
        if i < 12:
            source = part.at[m, c, :, d] if c % 2 == 0 else part.at[m, c, d]
            target = rb.at[m, i]
        else:
            source, target = tb.at[m, c, d], r2.at[m, i - 12]
        return remote(source, target, rs_s.at[m, i], rs_r.at[m, i], dev(way))

    def sum_landed(m, i):
        _, _, way = sum_way(i)
        target = rb.at[m, i] if i < 12 else r2.at[m, i - 12]
        remote(
            target, target, rs_s.at[m, i], rs_r.at[m, i], dev((-way[0], -way[1]))
        ).wait_recv()

    def hand_on(m):
        return remote(out.at[m], xin.at[m], x_s.at[m], x_r.at[m], (sec + 1, head))

    def modulate_and_send(m):
        @pl.when(first_section)
        def _():
            xin[m] = lat[pn[m]]

        @pl.when(sec > 0)
        def _():
            remote(xin.at[m], xin.at[m], x_s.at[m], x_r.at[m], (sec - 1, head)).wait_recv()

        values = xin[m].astype(F32)
        center = values - jnp.mean(values, axis=-1, keepdims=True)
        spread = jnp.mean(center * center, axis=-1, keepdims=True)
        normed = center * lax.rsqrt(spread + 1e-06)
        modded = (normed * (1.0 + scl[...]) + off[...]).astype(BF16)
        xg[m, A, 0] = modded[:, :1536]
        xg[m, B, 0] = modded[:, 1536:]
        for i in range(12):
            gather_copy(m, i).start()

    def gather_forward(m):
        for first, after in FORWARD:
            gather_landed(m, first)
            for i in after:
                gather_copy(m, i).start()
        for i in range(6, 12):
            gather_landed(m, i)

    def gather_rest(m):
        for i in range(12, len(GATHER)):
            gather_landed(m, i)

    def dot(a, b):
        return jnp.dot(a, b, preferred_element_type=F32)

    def dot_tn(a, b):
        return lax.dot_general(a, b, (((0,), (0,)), ((), ())), preferred_element_type=F32)

    def dot_nt(a, b):
        return lax.dot_general(a, b, (((1,), (1,)), ((), ())), preferred_element_type=F32)

    def merge(i, _):
        rows = pl.ds(pl.multiple_of(i * 256, 256), 256)
        down = dnt[:, rows]
        for n in range(3):
            win[rows, n * DH:(n + 1) * DH] = (
                win[rows, n * DH:(n + 1) * DH].astype(F32) + dot_tn(down, upq[n])
            ).astype(BF16)
            cols = slice(3 * DH + n * 256, 3 * DH + (n + 1) * 256)
            win[rows, cols] = (
                win[rows, cols].astype(F32) + dot_tn(down, upf[:, n * 256:(n + 1) * 256])
            ).astype(BF16)
        return 0

    def project(m, lo, hi):
        def tile(first, width):
            acc = None
            for hf in range(2):
                rows = xg[m, hf, lo // 16:hi // 16].reshape(hi - lo, 1536)
                term = dot(rows, win[hf * 1536:(hf + 1) * 1536, pl.ds(first, width)])
                acc = term if acc is None else acc + term
            return acc

        qkv[lo:hi, 0:256] = tile(0, 256)
        qkv[lo:hi, 256:384] = tile(256, DH)

        def feed(n, _):
            cols = pl.ds(pl.multiple_of(n * 256 + DH, DH), 256)
            acc = tile(pl.multiple_of(n * 256 + 3 * DH, DH), 256)
            act[lo:hi, cols] = jax.nn.gelu(acc, approximate=True).astype(BF16)
            return 0

        lax.fori_loop(0, 3, feed, 0)

    def attend(m):
        queries = rms_unit(qkv[:, 0:DH]).astype(BF16)
        fresh_keys = rms_unit(qkv[:, DH:2 * DH]).astype(BF16)
        fresh_values = qkv[:, 2 * DH:3 * DH].astype(BF16)
        for i in range(6, 12):
            stale_second_landed(m, i)
        total = jnp.zeros((256, 1), F32)
        mixed = jnp.zeros((256, DH), F32)
        for j in range(5):
            if j == 4:
                keys, values = fresh_keys, fresh_values
            else:
                keys = kv[m, 0, j].reshape(256, DH)
                values = kv[m, 1, :, j].reshape(256, DH)
            expo = jnp.exp(dot_nt(queries, keys) * (1.0 / math.sqrt(DH)))
            total += jnp.sum(expo, axis=-1, keepdims=True)
            mixed += dot(expo.astype(BF16), values)
        act[:, 0:DH] = (mixed / total).astype(BF16)

    def output_products(m):
        for c in range(4):
            for n in range(3):
                lo = c * 768 + n * 256
                term = dot(act[...], wout[:, lo:lo + 256]).astype(BF16)
                for k, place in enumerate(ORDER):
                    rows = term[k * 16:(k + 1) * 16]
                    part[m, c, place[0], place[1], :, n * 256:(n + 1) * 256] = rows
            for j in range(3):
                sum_copy(m, 3 * c + j).start()

    def wide(value):
        return value.astype(F32)

    def sum_up(m):
        for c in range(4):
            total = wide(part[m, c, :, 0] if c % 2 == 0 else part[m, c, 0])
            for j in range(3):
                sum_landed(m, 3 * c + j)
                total += wide(rb[m, 3 * c + j])
            tb[m, c] = total.astype(BF16)
            for j in range(3):
                sum_copy(m, 12 + 3 * c + j).start()
        for c in range(4):
            branch = wide(part[m, c, 0, 0])
            for j in range(3):
                branch += wide(rb[m, 3 * c + j, 0])
            for j in range(3):
                sum_landed(m, 12 + 3 * c + j)
                branch += wide(r2[m, 3 * c + j])
            cols = slice(c * 768, (c + 1) * 768)
            out[m, :, cols] = (wide(xin[m, :, cols]) + gate[:, cols] * branch).astype(BF16)

        @pl.when(sec < sections - 1)
        def _():
            hand_on(m).start()

    def stale_send_step(m, _):
        stale_send(m)
        return 0

    def stale_forward_step(m, _):
        stale_forward(m)
        return 0

    ahead = jnp.where(sec == 0, 0, jnp.where(sec == 1, 1, patches))
    w_copies[0].wait()
    lax.fori_loop(0, ahead, stale_send_step, 0)

    @pl.when(sec > 0)
    def _():
        for copy in w_copies[1:5]:
            copy.wait()

    lax.fori_loop(0, jnp.where(sec == 0, 0, 12), merge, 0)
    lax.fori_loop(0, ahead, stale_forward_step, 0)

    def patch(m, _):
        opening = jnp.logical_and(sec == 0, m == 0)
        more_stale = jnp.logical_and(sec < 2, m < patches - 1)
        modulate_and_send(m)

        @pl.when(opening)
        def _():
            stale_send(0)

        gather_forward(m)

        @pl.when(opening)
        def _():
            for copy in w_copies[1:5]:
                copy.wait()
            lax.fori_loop(0, 12, merge, 0)
            stale_forward(0)

        project(m, 0, EARLY)
        gather_rest(m)
        project(m, EARLY, 256)

        @pl.when(more_stale)
        def _():
            stale_send(m + 1)

        attend(m)

        @pl.when(m == 0)
        def _():
            for copy in w_copies[5:]:
                copy.wait()

        output_products(m)

        @pl.when(more_stale)
        def _():
            stale_forward(m + 1)

        sum_up(m)
        return 0

    lax.fori_loop(0, patches, patch, 0)

    def drain(m, _):
        for i in range(len(GATHER)):
            gather_copy(m, i).wait_send()
        for i in range(24):
            sum_copy(m, i).wait_send()
        for i in range(6):
            stale_first(m, i).wait_send()
        for i in range(6, 12):
            stale_second(m, i).wait_send()

        @pl.when(sec < sections - 1)
        def _():
            hand_on(m).wait_send()

        return 0

    lax.fori_loop(0, patches, drain, 0)


def per_device(
    latents, patch_numbers, prior_step_cache, old_block_index, modulation_offset, modulation_scale,
    modulation_gate, query_key_value_weight, feedforward_input_weight, adapter_down_weight,
    adapter_up_query_key_value, adapter_up_feedforward, attention_output_weight,
    feedforward_output_weight,
):
    patches = old_block_index.shape[1]
    vmem = pl.BlockSpec(memory_space=pltpu.VMEM)
    smem = pl.BlockSpec(memory_space=pltpu.SMEM)
    hbm = pl.BlockSpec(memory_space=pl.ANY)
    dma = pltpu.SemaphoreType.DMA
    record = pl.pallas_call(
        kernel,
        out_shape=jax.ShapeDtypeStruct((patches, 16, 3072), BF16),
        in_specs=[vmem, smem, smem] + [vmem] * 6 + [hbm] * 5,
        out_specs=vmem,
        scratch_shapes=[
            pltpu.VMEM((3072, 1152), BF16),
            pltpu.VMEM((896, 3072), BF16),
            pltpu.VMEM((2, 16, 16, 2048), BF16),
            pltpu.VMEM((patches, 2, 4, 4, 64, DH), BF16),
            pltpu.VMEM((patches, 2, 4, 4, 64, DH), BF16),
            pltpu.VMEM((patches, 2, 4, 4, 64, DH), BF16),
            pltpu.VMEM((patches, 16, 3072), BF16),
            pltpu.VMEM((patches, 2, 16, 16, 1536), BF16),
            pltpu.VMEM((256, 3 * DH), F32),
            pltpu.VMEM((256, 896), BF16),
            pltpu.VMEM((patches, 4, 4, 4, 16, 768), BF16),
            pltpu.VMEM((patches, 12, 4, 16, 768), BF16),
            pltpu.VMEM((patches, 4, 4, 16, 768), BF16),
            pltpu.VMEM((patches, 12, 16, 768), BF16),
            dma((patches, len(GATHER))),
            dma((patches, len(GATHER))),
            dma((patches, 24)),
            dma((patches, 24)),
            dma((patches, 12)),
            dma((patches, 12)),
            dma((patches,)),
            dma((patches,)),
            dma((7,)),
        ],
        compiler_params=pltpu.CompilerParams(
            collective_id=0, has_side_effects=True, vmem_limit_bytes=58 * 2**20
        ),
        cost_estimate=pl.CostEstimate(
            flops=10_000_000_000, bytes_accessed=16_000_000, transcendentals=2_000_000
        ),
    )(
        latents,
        patch_numbers,
        old_block_index[0],
        modulation_offset,
        modulation_scale,
        modulation_gate,
        adapter_up_query_key_value[0].transpose(1, 0, 2),
        adapter_up_feedforward[0],
        adapter_down_weight[0].T,
        prior_step_cache[0].transpose(2, 0, 1, 3),
        query_key_value_weight[0].transpose(1, 0, 2),
        feedforward_input_weight[0],
        attention_output_weight[0],
        feedforward_output_weight[0],
    )
    return record[None]


def solution(mesh):
    placed = (
        P(None, "head", None),
        P(),
        P("section", None, "head", None, None),
        P("section", None, None),
        P("section", None),
        P("section", None),
        P("section", None),
        P("section", None, None, "head"),
        P("section", None, "head"),
        P("section", None, None),
        P("section", None, None, "head"),
        P("section", None, "head"),
        P("section", "head", None),
        P("section", "head", None),
    )
    return jax.shard_map(
        per_device,
        mesh=mesh,
        in_specs=placed,
        out_specs=P("section", None, "head", None),
        check_vma=False,
    )
```

time: 412 us -> 327 us (0.79)
  Pallas kernels: 405 us -> 320 us
    pallas_call x1, Pallas kernels: 405 us -> 320 us  [per_device(): pl.pallas_call(kernel, out_shape=jax.ShapeDtypeStruct((patches, 16, 3072)...]
where the time goes in v2:
time: 327 us
  Pallas kernels  320 us (98%)
  local copies, waits for them, and re-layouts  6.77 us (2%)
    pallas_call x1, Pallas kernels, per_device(): pl.pallas_call(kernel, out_shape=jax.ShapeDtypeStruct((patches, 16, 3072)...  320 us
    unnamed x3, local copies, waits for them, and re-layouts  6.77 us

profile of v2, /device:TPU:97, one launch (start us, length us, event | category | flops | bytes accessed | tf_op | source)
XLA Modules:
  0.0 326.9 jit_solution(6458868911482516639)
XLA Ops:
  0.0 1.3 copy.20
  1.3 3.8 %copy.19 = bf16[1,16,16,2,2048]{4,2,1,3,0:T(8,128)(2,1)} copy(bf16[1,16,16,2,2048]{4,3,2,1,0:T(2,128)(2,1)} %param.16) | data formatting | bytes 4194304 | tf_op args[2]
  5.1 320.1 %shard_map.136 = bf16[3,16,3072]{2,1,0:T(8,128)(2,1)} custom-call(bf16[4,16,3072]{2,1,0:T(8,128)(2,1)} %lat.1, s32[3]{0:T(128)} %pn.1, s32[3,4]{1,0:T(4,128)} %bitcast.24, f32[1,3072]{1,0:T(1,128)} %off.1, f32[1,3072]{1,0:T(1,128)} %scl.1, f32[1,3072]{1,0:T(1,128)} %gate.1, bf16[3,64,128]{2,1,0:T(8,128)(2,1)} %bitcast.31, bf16[64,768]{1,0:T(8,128)(2,1)} %bitcast.30, ...), custom_call_target="tpu_custom_call" | custom-call | flops 10000000000 | bytes 16000000 | tf_op jit(solution)/shard_map/pallas_call | solution.py:433
  325.2 1.7 copy.22

commit v3 on v2

--- a/solution.py
+++ b/solution.py
@@ -82,8 +82,7 @@
         pltpu.make_async_copy(woa_hbm, wout.at[pl.ds(0, DH)], w_sem.at[5]),
         pltpu.make_async_copy(wof_hbm, wout.at[pl.ds(DH, 768)], w_sem.at[6]),
     ]
-    for copy in w_copies:
-        copy.start()
+    w_copies[0].start()
 
     barrier = pltpu.get_barrier_semaphore()
     for d in FAR_FIRST:
@@ -156,9 +155,10 @@
 
     def stale_send(m):
         def one(j, _):
-            block = bidx[m, j]
-            keys = cachev[0, block].astype(F32)
-            values = cachev[1, block]
+            block = bidx[m, 0, j]
+            both = cachev[block]
+            keys = both[:, 0].astype(F32)
+            values = both[:, 1]
             rows = pl.ds(pl.multiple_of(j * 16, 16), 16)
             for h in range(16):
                 part_k = keys[:, h * DH:(h + 1) * DH]
@@ -204,8 +204,15 @@
             target, target, rs_s.at[m, i], rs_r.at[m, i], dev((-way[0], -way[1]))
         ).wait_recv()
 
-    def hand_on(m):
-        return remote(out.at[m], xin.at[m], x_s.at[m], x_r.at[m], (sec + 1, head))
+    def hand_on(m, c):
+        cols = pl.ds(c * 768, 768)
+        return remote(
+            out.at[m, :, cols], xin.at[m, :, cols], x_s.at[m, c], x_r.at[m, c], (sec + 1, head)
+        )
+
+    def handed(m, c):
+        ref = xin.at[m, :, pl.ds(c * 768, 768)]
+        remote(ref, ref, x_s.at[m, c], x_r.at[m, c], (sec - 1, head)).wait_recv()
 
     def modulate_and_send(m):
         @pl.when(first_section)
@@ -214,7 +221,8 @@
 
         @pl.when(sec > 0)
         def _():
-            remote(xin.at[m], xin.at[m], x_s.at[m], x_r.at[m], (sec - 1, head)).wait_recv()
+            for c in range(4):
+                handed(m, c)
 
         values = xin[m].astype(F32)
         center = values - jnp.mean(values, axis=-1, keepdims=True)
@@ -280,24 +288,27 @@
 
         lax.fori_loop(0, 3, feed, 0)
 
-    def attend(m):
-        queries = rms_unit(qkv[:, 0:DH]).astype(BF16)
-        fresh_keys = rms_unit(qkv[:, DH:2 * DH]).astype(BF16)
-        fresh_values = qkv[:, 2 * DH:3 * DH].astype(BF16)
-        for i in range(6, 12):
-            stale_second_landed(m, i)
-        total = jnp.zeros((256, 1), F32)
-        mixed = jnp.zeros((256, DH), F32)
-        for j in range(5):
-            if j == 4:
-                keys, values = fresh_keys, fresh_values
-            else:
-                keys = kv[m, 0, j].reshape(256, DH)
-                values = kv[m, 1, :, j].reshape(256, DH)
-            expo = jnp.exp(dot_nt(queries, keys) * (1.0 / math.sqrt(DH)))
-            total += jnp.sum(expo, axis=-1, keepdims=True)
-            mixed += dot(expo.astype(BF16), values)
-        act[:, 0:DH] = (mixed / total).astype(BF16)
+    def attend_to(queries, keys, values, state):
+        expo = jnp.exp(dot_nt(queries, keys) * (1.0 / math.sqrt(DH)))
+        total = jnp.sum(expo, axis=-1, keepdims=True)
+        mixed = dot(expo.astype(BF16), values)
+        return (mixed, total) if state is None else (state[0] + mixed, state[1] + total)
+
+    def attend_cached(m, lo, hi):
+        queries = rms_unit(qkv[lo:hi, 0:DH]).astype(BF16)
+        state = None
+        for j in range(4):
+            keys = kv[m, 0, j].reshape(256, DH)
+            values = kv[m, 1, :, j].reshape(256, DH)
+            state = attend_to(queries, keys, values, state)
+        return queries, state
+
+    def attend_fresh(early, late):
+        keys = rms_unit(qkv[:, DH:2 * DH]).astype(BF16)
+        values = qkv[:, 2 * DH:3 * DH].astype(BF16)
+        for lo, hi, (queries, state) in ((0, EARLY, early), (EARLY, 256, late)):
+            mixed, total = attend_to(queries, keys, values, state)
+            act[lo:hi, 0:DH] = (mixed / total).astype(BF16)
 
     def output_products(m):
         for c in range(4):
@@ -332,9 +343,9 @@
             cols = slice(c * 768, (c + 1) * 768)
             out[m, :, cols] = (wide(xin[m, :, cols]) + gate[:, cols] * branch).astype(BF16)
 
-        @pl.when(sec < sections - 1)
-        def _():
-            hand_on(m).start()
+            @pl.when(sec < sections - 1)
+            def _():
+                hand_on(m, c).start()
 
     def stale_send_step(m, _):
         stale_send(m)
@@ -344,25 +355,26 @@
         stale_forward(m)
         return 0
 
-    ahead = jnp.where(sec == 0, 0, jnp.where(sec == 1, 1, patches))
-    w_copies[0].wait()
-    lax.fori_loop(0, ahead, stale_send_step, 0)
-
     @pl.when(sec > 0)
     def _():
+        w_copies[0].wait()
+        for copy in w_copies[1:]:
+            copy.start()
+        lax.fori_loop(0, patches, stale_send_step, 0)
         for copy in w_copies[1:5]:
             copy.wait()
-
-    lax.fori_loop(0, jnp.where(sec == 0, 0, 12), merge, 0)
-    lax.fori_loop(0, ahead, stale_forward_step, 0)
+        lax.fori_loop(0, 12, merge, 0)
+        lax.fori_loop(0, patches, stale_forward_step, 0)
 
     def patch(m, _):
         opening = jnp.logical_and(sec == 0, m == 0)
-        more_stale = jnp.logical_and(sec < 2, m < patches - 1)
         modulate_and_send(m)
 
         @pl.when(opening)
         def _():
+            w_copies[0].wait()
+            for copy in w_copies[1:]:
+                copy.start()
             stale_send(0)
 
         gather_forward(m)
@@ -375,14 +387,18 @@
             stale_forward(0)
 
         project(m, 0, EARLY)
+        for i in range(6, 12):
+            stale_second_landed(m, i)
+        early = attend_cached(m, 0, EARLY)
         gather_rest(m)
         project(m, EARLY, 256)
 
-        @pl.when(more_stale)
-        def _():
-            stale_send(m + 1)
-
-        attend(m)
+        @pl.when(opening)
+        def _():
+            lax.fori_loop(1, patches, stale_send_step, 0)
+
+        late = attend_cached(m, EARLY, 256)
+        attend_fresh(early, late)
 
         @pl.when(m == 0)
         def _():
@@ -391,9 +407,9 @@
 
         output_products(m)
 
-        @pl.when(more_stale)
-        def _():
-            stale_forward(m + 1)
+        @pl.when(opening)
+        def _():
+            lax.fori_loop(1, patches, stale_forward_step, 0)
 
         sum_up(m)
         return 0
@@ -412,7 +428,8 @@
 
         @pl.when(sec < sections - 1)
         def _():
-            hand_on(m).wait_send()
+            for c in range(4):
+                hand_on(m, c).wait_send()
 
         return 0
 
@@ -438,7 +455,7 @@
         scratch_shapes=[
             pltpu.VMEM((3072, 1152), BF16),
             pltpu.VMEM((896, 3072), BF16),
-            pltpu.VMEM((2, 16, 16, 2048), BF16),
+            pltpu.VMEM((16, 16, 2, 2048), BF16),
             pltpu.VMEM((patches, 2, 4, 4, 64, DH), BF16),
             pltpu.VMEM((patches, 2, 4, 4, 64, DH), BF16),
             pltpu.VMEM((patches, 2, 4, 4, 64, DH), BF16),
@@ -456,8 +473,8 @@
             dma((patches, 24)),
             dma((patches, 12)),
             dma((patches, 12)),
-            dma((patches,)),
-            dma((patches,)),
+            dma((patches, 4)),
+            dma((patches, 4)),
             dma((7,)),
         ],
         compiler_params=pltpu.CompilerParams(
@@ -469,14 +486,14 @@
     )(
         latents,
         patch_numbers,
-        old_block_index[0],
+        old_block_index.transpose(1, 0, 2),
         modulation_offset,
         modulation_scale,
         modulation_gate,
         adapter_up_query_key_value[0].transpose(1, 0, 2),
         adapter_up_feedforward[0],
         adapter_down_weight[0].T,
-        prior_step_cache[0].transpose(2, 0, 1, 3),
+        prior_step_cache[0],
         query_key_value_weight[0].transpose(1, 0, 2),
         feedforward_input_weight[0],
         attention_output_weight[0],

time: 327 us -> 327 us (level)
  local copies, waits for them, and re-layouts: 6.77 us -> 1.69 us
  Pallas kernels: 320 us -> 325 us
    pallas_call x1, Pallas kernels: 320 us -> 325 us  [per_device(): pl.pallas_call(kernel, out_shape=jax.ShapeDtypeStruct((patches, 16, 3072)...]
    unnamed x3 -> x1, local copies, waits for them, and re-layouts: 6.77 us -> 1.69 us
where the time goes in v3:
time: 327 us
  Pallas kernels  325 us (99%)
    pallas_call x1, Pallas kernels, per_device(): pl.pallas_call(kernel, out_shape=jax.ShapeDtypeStruct((patches, 16, 3072)...  325 us

profile of v3, /device:TPU:97, one launch (start us, length us, event | category | flops | bytes accessed | tf_op | source)
XLA Modules:
  0.0 327.1 jit_solution(13062689645248983167)
XLA Ops:
  0.0 325.4 %shard_map.136 = bf16[3,16,3072]{2,1,0:T(8,128)(2,1)} custom-call(bf16[4,16,3072]{2,1,0:T(8,128)(2,1)} %lat.1, s32[3]{0:T(128)} %pn.1, s32[3,1,4]{2,1,0:T(1,128)} %bitcast.25, f32[1,3072]{1,0:T(1,128)} %off.1, f32[1,3072]{1,0:T(1,128)} %scl.1, f32[1,3072]{1,0:T(1,128)} %gate.1, bf16[3,64,128]{2,1,0:T(8,128)(2,1)} %bitcast.24, bf16[64,768]{1,0:T(8,128)(2,1)} %bitcast.23, ...), custom_call_target="tpu_custom_call" | custom-call | flops 10000000000 | bytes 16000000 | tf_op jit(solution)/shard_map/pallas_call | solution.py:450
  325.4 1.7 copy.16

commit v4 on v3

--- a/solution.py
+++ b/solution.py
@@ -49,10 +49,12 @@
 
 
 def kernel(
-    lat, pn, bidx, off, scl, gate, upq, upf, dnt, cache_hbm, wqkv_hbm, wffn_hbm, woa_hbm, wof_hbm,
+    pn, bidx, lat_hbm, off_hbm, scl_hbm, gate_hbm, upq_hbm, upf_hbm, dnt_hbm, cache_hbm, wqkv_hbm,
+    wffn_hbm, woa_hbm, wof_hbm,
     out,
+    lat, off, scl, gate, upq, upf, dnt,
     win, wout, cachev, skv, r1, kv, xin, xg, qkv, act, part, rb, tb, r2,
-    ag_s, ag_r, rs_s, rs_r, st_s, st_r, x_s, x_r, w_sem,
+    ag_s, ag_r, rs_s, rs_r, st_s, st_r, x_s, x_r, w_sem, turn,
 ):
     patches = xin.shape[0]
     sections = lax.axis_size("section")
@@ -82,7 +84,23 @@
         pltpu.make_async_copy(woa_hbm, wout.at[pl.ds(0, DH)], w_sem.at[5]),
         pltpu.make_async_copy(wof_hbm, wout.at[pl.ds(DH, 768)], w_sem.at[6]),
     ]
+    v_copies = [
+        pltpu.make_async_copy(source, target, w_sem.at[7 + i])
+        for i, (source, target) in enumerate((
+            (off_hbm, off), (scl_hbm, scl), (gate_hbm, gate), (upq_hbm, upq), (upf_hbm, upf),
+            (dnt_hbm, dnt), (lat_hbm, lat),
+        ))
+    ]
+
+    @pl.when(first_section)
+    def _():
+        v_copies[6].start()
+
+    for copy in v_copies[:3]:
+        copy.start()
     w_copies[0].start()
+    for copy in v_copies[3:6]:
+        copy.start()
 
     barrier = pltpu.get_barrier_semaphore()
     for d in FAR_FIRST:
@@ -361,13 +379,29 @@
         for copy in w_copies[1:]:
             copy.start()
         lax.fori_loop(0, patches, stale_send_step, 0)
-        for copy in w_copies[1:5]:
+        for copy in w_copies[1:5] + v_copies[:6]:
             copy.wait()
         lax.fori_loop(0, 12, merge, 0)
         lax.fori_loop(0, patches, stale_forward_step, 0)
 
+    @pl.when(first_section)
+    def _():
+        for copy in v_copies[:3] + v_copies[6:]:
+            copy.wait()
+
+    def await_turn(m):
+        @pl.when(jnp.logical_and(lax.rem(sec, 2) == 0, m > 0))
+        def _():
+            pl.semaphore_wait(turn, 1)
+
+    def give_turn(m):
+        @pl.when(jnp.logical_and(lax.rem(sec, 2) == 1, m < patches - 1))
+        def _():
+            pl.semaphore_signal(turn, inc=1, device_id=(sec - 1, head), device_id_type=MESH)
+
     def patch(m, _):
         opening = jnp.logical_and(sec == 0, m == 0)
+        await_turn(m)
         modulate_and_send(m)
 
         @pl.when(opening)
@@ -378,10 +412,11 @@
             stale_send(0)
 
         gather_forward(m)
+        give_turn(m)
 
         @pl.when(opening)
         def _():
-            for copy in w_copies[1:5]:
+            for copy in w_copies[1:5] + v_copies[3:6]:
                 copy.wait()
             lax.fori_loop(0, 12, merge, 0)
             stale_forward(0)
@@ -450,9 +485,16 @@
     record = pl.pallas_call(
         kernel,
         out_shape=jax.ShapeDtypeStruct((patches, 16, 3072), BF16),
-        in_specs=[vmem, smem, smem] + [vmem] * 6 + [hbm] * 5,
+        in_specs=[smem, smem] + [hbm] * 12,
         out_specs=vmem,
         scratch_shapes=[
+            pltpu.VMEM(latents.shape, BF16),
+            pltpu.VMEM((1, 3072), F32),
+            pltpu.VMEM((1, 3072), F32),
+            pltpu.VMEM((1, 3072), F32),
+            pltpu.VMEM((3, 64, DH), BF16),
+            pltpu.VMEM((64, 768), BF16),
+            pltpu.VMEM((64, 3072), BF16),
             pltpu.VMEM((3072, 1152), BF16),
             pltpu.VMEM((896, 3072), BF16),
             pltpu.VMEM((16, 16, 2, 2048), BF16),
@@ -475,7 +517,8 @@
             dma((patches, 12)),
             dma((patches, 4)),
             dma((patches, 4)),
-            dma((7,)),
+            dma((14,)),
+            pltpu.SemaphoreType.REGULAR,
         ],
         compiler_params=pltpu.CompilerParams(
             collective_id=0, has_side_effects=True, vmem_limit_bytes=58 * 2**20
@@ -484,9 +527,9 @@
             flops=10_000_000_000, bytes_accessed=16_000_000, transcendentals=2_000_000
         ),
     )(
-        latents,
         patch_numbers,
         old_block_index.transpose(1, 0, 2),
+        latents,
         modulation_offset,
         modulation_scale,
         modulation_gate,

time: 327 us -> 309 us (0.945)
  Pallas kernels: 325 us -> 307 us
    pallas_call x1, Pallas kernels: 325 us -> 307 us  [per_device(): pl.pallas_call(kernel, out_shape=jax.ShapeDtypeStruct((patches, 16, 3072)...]
where the time goes in v4:
time: 309 us
  Pallas kernels  307 us (99%)
    pallas_call x1, Pallas kernels, per_device(): pl.pallas_call(kernel, out_shape=jax.ShapeDtypeStruct((patches, 16, 3072)...  307 us

profile of v4, /device:TPU:97, one launch (start us, length us, event | category | flops | bytes accessed | tf_op | source)
XLA Modules:
  0.0 308.9 jit_solution(11258865281005763721)
XLA Ops:
  0.0 307.2 %shard_map.136 = bf16[3,16,3072]{2,1,0:T(8,128)(2,1)} custom-call(s32[3]{0:T(128)} %pn.1, s32[3,1,4]{2,1,0:T(1,128)} %bitcast.25, bf16[4,16,3072]{2,1,0:T(8,128)(2,1)} %lat_hbm.1, f32[1,3072]{1,0:T(1,128)} %off_hbm.1, f32[1,3072]{1,0:T(1,128)} %scl_hbm.1, f32[1,3072]{1,0:T(1,128)} %gate_hbm.1, bf16[3,64,128]{2,1,0:T(8,128)(2,1)} %bitcast.24, ...), custom_call_target="tpu_custom_call" | custom-call | flops 10000000000 | bytes 16000000 | tf_op jit(solution)/shard_map/pallas_call | solution.py:485
  307.2 1.7 copy.16

commit v5 on v4

--- a/solution.py
+++ b/solution.py
@@ -52,9 +52,9 @@
     pn, bidx, lat_hbm, off_hbm, scl_hbm, gate_hbm, upq_hbm, upf_hbm, dnt_hbm, cache_hbm, wqkv_hbm,
     wffn_hbm, woa_hbm, wof_hbm,
     out,
-    lat, off, scl, gate, upq, upf, dnt,
+    lat, off, scl, gate, upq, upf, dnt, next_off, next_scl, ahead,
     win, wout, cachev, skv, r1, kv, xin, xg, qkv, act, part, rb, tb, r2,
-    ag_s, ag_r, rs_s, rs_r, st_s, st_r, x_s, x_r, w_sem, turn,
+    ag_s, ag_r, rs_s, rs_r, st_s, st_r, x_s, x_r, w_sem, turn, nx_s, nm_s, nm_r,
 ):
     patches = xin.shape[0]
     sections = lax.axis_size("section")
@@ -73,7 +73,8 @@
         return (sec, px(d[0]) * 4 + py(d[1]))
 
     first_section = sec == 0
-    last_section = sec == sections - 1
+    even = lax.rem(sec, 2) == 0
+    odd = lax.rem(sec, 2) == 1
 
     w_copies = [
         pltpu.make_async_copy(cache_hbm, cachev, w_sem.at[0]),
@@ -111,7 +112,16 @@
     for step in (1, sections - 1):
         neighbour = (lax.rem(sec + step, sections), head)
         pl.semaphore_signal(barrier, inc=1, device_id=neighbour, device_id_type=MESH)
-    pl.semaphore_wait(barrier, 8)
+
+    @pl.when(odd)
+    def _():
+        for d in FAR_FIRST:
+            for axis in (0, 1):
+                way = along(axis, d)
+                peer = (sec - 1, px(way[0]) * 4 + py(way[1]))
+                pl.semaphore_signal(barrier, inc=1, device_id=peer, device_id_type=MESH)
+
+    pl.semaphore_wait(barrier, jnp.where(even, 14, 8))
 
     def remote(src, dst, ssem, rsem, device):
         return pltpu.make_async_remote_copy(
@@ -125,6 +135,26 @@
         return remote(
             xg.at[m, hf, slot(place)], xg.at[m, hf, there], ag_s.at[m, i], ag_r.at[m, i], dev(way)
         )
+
+    def next_copy(m, i):
+        if i == 12:
+            return remote(
+                ahead.at[m], xg.at[m, :, 0], nx_s.at[m, 12], ag_r.at[m, len(GATHER)], (sec + 1, head)
+            )
+        hf, _, way = GATHER[i]
+        there = slot((-way[0], -way[1]))
+        target = (sec + 1, px(way[0]) * 4 + py(way[1]))
+        return remote(
+            ahead.at[m, hf], xg.at[m, hf, there], nx_s.at[m, i], ag_r.at[m, i], target
+        )
+
+    def own_landed(m):
+        ref = xg.at[m, :, 0]
+        remote(ref, ref, nx_s.at[m, 12], ag_r.at[m, len(GATHER)], (sec - 1, head)).wait_recv()
+
+    def modulation_copy(i):
+        source, target = ((off, next_off), (scl, next_scl))[i]
+        return remote(source, target, nm_s.at[i], nm_r.at[i], (sec - 1, head))
 
     def gather_landed(m, i):
         hf, place, way = GATHER[i]
@@ -232,21 +262,24 @@
         ref = xin.at[m, :, pl.ds(c * 768, 768)]
         remote(ref, ref, x_s.at[m, c], x_r.at[m, c], (sec - 1, head)).wait_recv()
 
-    def modulate_and_send(m):
-        @pl.when(first_section)
-        def _():
-            xin[m] = lat[pn[m]]
-
-        @pl.when(sec > 0)
-        def _():
-            for c in range(4):
-                handed(m, c)
-
-        values = xin[m].astype(F32)
+    def modulated(rows, scale, offset):
+        values = rows.astype(F32)
         center = values - jnp.mean(values, axis=-1, keepdims=True)
         spread = jnp.mean(center * center, axis=-1, keepdims=True)
         normed = center * lax.rsqrt(spread + 1e-06)
-        modded = (normed * (1.0 + scl[...]) + off[...]).astype(BF16)
+        return (normed * (1.0 + scale[...]) + offset[...]).astype(BF16)
+
+    def modulate_and_send(m):
+        @pl.when(first_section)
+        def _():
+            xin[m] = lat[pn[m]]
+
+        @pl.when(sec > 0)
+        def _():
+            for c in range(4):
+                handed(m, c)
+
+        modded = modulated(xin[m], scl, off)
         xg[m, A, 0] = modded[:, :1536]
         xg[m, B, 0] = modded[:, 1536:]
         for i in range(12):
@@ -358,11 +391,34 @@
             for j in range(3):
                 sum_landed(m, 12 + 3 * c + j)
                 branch += wide(r2[m, 3 * c + j])
+
+            @pl.when(odd)
+            def _():
+                handed(m, c)
+
             cols = slice(c * 768, (c + 1) * 768)
             out[m, :, cols] = (wide(xin[m, :, cols]) + gate[:, cols] * branch).astype(BF16)
 
-            @pl.when(sec < sections - 1)
+            @pl.when(jnp.logical_and(odd, sec < sections - 1))
             def _():
+                hand_on(m, c).start()
+
+        @pl.when(even)
+        def _():
+            @pl.when(m == 0)
+            def _():
+                for i in range(2):
+                    source = (next_off, next_scl)[i]
+                    remote(
+                        source, source, nm_s.at[i], nm_r.at[i], (sec + 1, head)
+                    ).wait_recv()
+
+            modded = modulated(out[m], next_scl, next_off)
+            ahead[m, A] = modded[:, :1536]
+            ahead[m, B] = modded[:, 1536:]
+            for i in range(13):
+                next_copy(m, i).start()
+            for c in range(4):
                 hand_on(m, c).start()
 
     def stale_send_step(m, _):
@@ -372,6 +428,14 @@
     def stale_forward_step(m, _):
         stale_forward(m)
         return 0
+
+    for copy in v_copies[:3]:
+        copy.wait()
+
+    @pl.when(odd)
+    def _():
+        for i in range(2):
+            modulation_copy(i).start()
 
     @pl.when(sec > 0)
     def _():
@@ -379,18 +443,17 @@
         for copy in w_copies[1:]:
             copy.start()
         lax.fori_loop(0, patches, stale_send_step, 0)
-        for copy in w_copies[1:5] + v_copies[:6]:
+        for copy in w_copies[1:5] + v_copies[3:6]:
             copy.wait()
         lax.fori_loop(0, 12, merge, 0)
         lax.fori_loop(0, patches, stale_forward_step, 0)
 
     @pl.when(first_section)
     def _():
-        for copy in v_copies[:3] + v_copies[6:]:
-            copy.wait()
+        v_copies[6].wait()
 
     def await_turn(m):
-        @pl.when(jnp.logical_and(lax.rem(sec, 2) == 0, m > 0))
+        @pl.when(m > 0)
         def _():
             pl.semaphore_wait(turn, 1)
 
@@ -401,8 +464,11 @@
 
     def patch(m, _):
         opening = jnp.logical_and(sec == 0, m == 0)
-        await_turn(m)
-        modulate_and_send(m)
+
+        @pl.when(even)
+        def _():
+            await_turn(m)
+            modulate_and_send(m)
 
         @pl.when(opening)
         def _():
@@ -420,6 +486,10 @@
                 copy.wait()
             lax.fori_loop(0, 12, merge, 0)
             stale_forward(0)
+
+        @pl.when(odd)
+        def _():
+            own_landed(m)
 
         project(m, 0, EARLY)
         for i in range(6, 12):
@@ -452,7 +522,14 @@
     lax.fori_loop(0, patches, patch, 0)
 
     def drain(m, _):
-        for i in range(len(GATHER)):
+        @pl.when(even)
+        def _():
+            for i in range(12):
+                gather_copy(m, i).wait_send()
+            for i in range(13):
+                next_copy(m, i).wait_send()
+
+        for i in range(12, len(GATHER)):
             gather_copy(m, i).wait_send()
         for i in range(24):
             sum_copy(m, i).wait_send()
@@ -469,6 +546,11 @@
         return 0
 
     lax.fori_loop(0, patches, drain, 0)
+
+    @pl.when(odd)
+    def _():
+        for i in range(2):
+            modulation_copy(i).wait_send()
 
 
 def per_device(
@@ -495,6 +577,9 @@
             pltpu.VMEM((3, 64, DH), BF16),
             pltpu.VMEM((64, 768), BF16),
             pltpu.VMEM((64, 3072), BF16),
+            pltpu.VMEM((1, 3072), F32),
+            pltpu.VMEM((1, 3072), F32),
+            pltpu.VMEM((patches, 2, 16, 1536), BF16),
             pltpu.VMEM((3072, 1152), BF16),
             pltpu.VMEM((896, 3072), BF16),
             pltpu.VMEM((16, 16, 2, 2048), BF16),
@@ -510,7 +595,7 @@
             pltpu.VMEM((patches, 4, 4, 16, 768), BF16),
             pltpu.VMEM((patches, 12, 16, 768), BF16),
             dma((patches, len(GATHER))),
-            dma((patches, len(GATHER))),
+            dma((patches, len(GATHER) + 1)),
             dma((patches, 24)),
             dma((patches, 24)),
             dma((patches, 12)),
@@ -519,6 +604,9 @@
             dma((patches, 4)),
             dma((14,)),
             pltpu.SemaphoreType.REGULAR,
+            dma((patches, 13)),
+            dma((2,)),
+            dma((2,)),
         ],
         compiler_params=pltpu.CompilerParams(
             collective_id=0, has_side_effects=True, vmem_limit_bytes=58 * 2**20

time: 309 us -> 307 us (level)
  no operation moved by 1% of the time
where the time goes in v5:
time: 307 us; the launch traced here: 306 us
  Pallas kernels  305 us (99%)
    pallas_call x1, Pallas kernels, per_device(): pl.pallas_call(kernel, out_shape=jax.ShapeDtypeStruct((patches, 16, 3072)...  305 us

profile of v5, /device:TPU:97, one launch (start us, length us, event | category | flops | bytes accessed | tf_op | source)
XLA Modules:
  0.0 306.4 jit_solution(15681936086691640157)
XLA Ops:
  0.0 304.7 %shard_map.136 = bf16[3,16,3072]{2,1,0:T(8,128)(2,1)} custom-call(s32[3]{0:T(128)} %pn.1, s32[3,1,4]{2,1,0:T(1,128)} %bitcast.25, bf16[4,16,3072]{2,1,0:T(8,128)(2,1)} %lat_hbm.1, f32[1,3072]{1,0:T(1,128)} %off_hbm.1, f32[1,3072]{1,0:T(1,128)} %scl_hbm.1, f32[1,3072]{1,0:T(1,128)} %gate_hbm.1, bf16[3,64,128]{2,1,0:T(8,128)(2,1)} %bitcast.24, ...), custom_call_target="tpu_custom_call" | custom-call | flops 10000000000 | bytes 16000000 | tf_op jit(solution)/shard_map/pallas_call | solution.py:567
  304.7 1.7 copy.16

commit v6 on v5

--- a/solution.py
+++ b/solution.py
@@ -331,13 +331,13 @@
         qkv[lo:hi, 0:256] = tile(0, 256)
         qkv[lo:hi, 256:384] = tile(256, DH)
 
-        def feed(n, _):
-            cols = pl.ds(pl.multiple_of(n * 256 + DH, DH), 256)
-            acc = tile(pl.multiple_of(n * 256 + 3 * DH, DH), 256)
-            act[lo:hi, cols] = jax.nn.gelu(acc, approximate=True).astype(BF16)
-            return 0
-
-        lax.fori_loop(0, 3, feed, 0)
+        def feed():
+            for n in range(3):
+                acc = tile(n * 256 + 3 * DH, 256)
+                cols = slice(n * 256 + DH, (n + 1) * 256 + DH)
+                act[lo:hi, cols] = jax.nn.gelu(acc, approximate=True).astype(BF16)
+
+        return feed
 
     def attend_to(queries, keys, values, state):
         expo = jnp.exp(dot_nt(queries, keys) * (1.0 / math.sqrt(DH)))
@@ -491,18 +491,19 @@
         def _():
             own_landed(m)
 
-        project(m, 0, EARLY)
+        project(m, 0, EARLY)()
         for i in range(6, 12):
             stale_second_landed(m, i)
         early = attend_cached(m, 0, EARLY)
         gather_rest(m)
-        project(m, EARLY, 256)
 
         @pl.when(opening)
         def _():
             lax.fori_loop(1, patches, stale_send_step, 0)
 
+        feed = project(m, EARLY, 256)
         late = attend_cached(m, EARLY, 256)
+        feed()
         attend_fresh(early, late)
 
         @pl.when(m == 0)

time: 307 us -> 302 us (0.984)
  Pallas kernels: 305 us -> 300 us
    pallas_call x1, Pallas kernels: 305 us -> 300 us  [per_device(): pl.pallas_call(kernel, out_shape=jax.ShapeDtypeStruct((patches, 16, 3072)...]
where the time goes in v6:
time: 302 us; the launch traced here: 301 us
  Pallas kernels  300 us (99%)
    pallas_call x1, Pallas kernels, per_device(): pl.pallas_call(kernel, out_shape=jax.ShapeDtypeStruct((patches, 16, 3072)...  300 us

profile of v6, /device:TPU:97, one launch (start us, length us, event | category | flops | bytes accessed | tf_op | source)
XLA Modules:
  0.0 301.4 jit_solution(16438351616275189926)
XLA Ops:
  0.0 299.7 %shard_map.136 = bf16[3,16,3072]{2,1,0:T(8,128)(2,1)} custom-call(s32[3]{0:T(128)} %pn.1, s32[3,1,4]{2,1,0:T(1,128)} %bitcast.25, bf16[4,16,3072]{2,1,0:T(8,128)(2,1)} %lat_hbm.1, f32[1,3072]{1,0:T(1,128)} %off_hbm.1, f32[1,3072]{1,0:T(1,128)} %scl_hbm.1, f32[1,3072]{1,0:T(1,128)} %gate_hbm.1, bf16[3,64,128]{2,1,0:T(8,128)(2,1)} %bitcast.24, ...), custom_call_target="tpu_custom_call" | custom-call | flops 10000000000 | bytes 16000000 | tf_op jit(solution)/shard_map/pallas_call | solution.py:568
  299.7 1.7 copy.16

commit v7 on v6

--- a/solution.py
+++ b/solution.py
@@ -286,8 +286,10 @@
             gather_copy(m, i).start()
 
     def gather_forward(m):
-        for first, after in FORWARD:
+        for k, (first, after) in enumerate(FORWARD):
             gather_landed(m, first)
+            if k == 5:
+                give_turn(m)
             for i in after:
                 gather_copy(m, i).start()
         for i in range(6, 12):
@@ -462,6 +464,33 @@
         def _():
             pl.semaphore_signal(turn, inc=1, device_id=(sec - 1, head), device_id_type=MESH)
 
+    def drain_early(m):
+        @pl.when(even)
+        def _():
+            for i in range(12):
+                gather_copy(m, i).wait_send()
+
+        for i in range(12, len(GATHER)):
+            gather_copy(m, i).wait_send()
+        for i in range(6):
+            stale_first(m, i).wait_send()
+        for i in range(6, 12):
+            stale_second(m, i).wait_send()
+
+    def drain_late(m):
+        for i in range(24):
+            sum_copy(m, i).wait_send()
+
+        @pl.when(even)
+        def _():
+            for i in range(13):
+                next_copy(m, i).wait_send()
+
+        @pl.when(sec < sections - 1)
+        def _():
+            for c in range(4):
+                hand_on(m, c).wait_send()
+
     def patch(m, _):
         opening = jnp.logical_and(sec == 0, m == 0)
 
@@ -478,7 +507,6 @@
             stale_send(0)
 
         gather_forward(m)
-        give_turn(m)
 
         @pl.when(opening)
         def _():
@@ -517,36 +545,18 @@
         def _():
             lax.fori_loop(1, patches, stale_forward_step, 0)
 
+        drain_early(m)
+
+        @pl.when(m > 0)
+        def _():
+            drain_late(m - 1)
+
         sum_up(m)
         return 0
 
     lax.fori_loop(0, patches, patch, 0)
 
-    def drain(m, _):
-        @pl.when(even)
-        def _():
-            for i in range(12):
-                gather_copy(m, i).wait_send()
-            for i in range(13):
-                next_copy(m, i).wait_send()
-
-        for i in range(12, len(GATHER)):
-            gather_copy(m, i).wait_send()
-        for i in range(24):
-            sum_copy(m, i).wait_send()
-        for i in range(6):
-            stale_first(m, i).wait_send()
-        for i in range(6, 12):
-            stale_second(m, i).wait_send()
-
-        @pl.when(sec < sections - 1)
-        def _():
-            for c in range(4):
-                hand_on(m, c).wait_send()
-
-        return 0
-
-    lax.fori_loop(0, patches, drain, 0)
+    drain_late(patches - 1)
 
     @pl.when(odd)
     def _():

time: 302 us -> 301 us (level)
  no operation moved by 1% of the time
where the time goes in v7:
time: 301 us
  Pallas kernels  300 us (100%)
    pallas_call x1, Pallas kernels, per_device(): pl.pallas_call(kernel, out_shape=jax.ShapeDtypeStruct((patches, 16, 3072)...  300 us

profile of v7, /device:TPU:97, one launch (start us, length us, event | category | flops | bytes accessed | tf_op | source)
XLA Modules:
  0.0 301.2 jit_solution(5373873795725651137)
XLA Ops:
  0.0 299.5 %shard_map.136 = bf16[3,16,3072]{2,1,0:T(8,128)(2,1)} custom-call(s32[3]{0:T(128)} %pn.1, s32[3,1,4]{2,1,0:T(1,128)} %bitcast.25, bf16[4,16,3072]{2,1,0:T(8,128)(2,1)} %lat_hbm.1, f32[1,3072]{1,0:T(1,128)} %off_hbm.1, f32[1,3072]{1,0:T(1,128)} %scl_hbm.1, f32[1,3072]{1,0:T(1,128)} %gate_hbm.1, bf16[3,64,128]{2,1,0:T(8,128)(2,1)} %bitcast.24, ...), custom_call_target="tpu_custom_call" | custom-call | flops 10000000000 | bytes 16000000 | tf_op jit(solution)/shard_map/pallas_call | solution.py:578
  299.5 1.7 copy.16

commit v8 on v6

--- a/solution.py
+++ b/solution.py
@@ -384,6 +384,11 @@
             tb[m, c] = total.astype(BF16)
             for j in range(3):
                 sum_copy(m, 12 + 3 * c + j).start()
+        @pl.when(odd)
+        def _():
+            for c in range(4):
+                handed(m, c)
+
         for c in range(4):
             branch = wide(part[m, c, 0, 0])
             for j in range(3):
@@ -391,11 +396,6 @@
             for j in range(3):
                 sum_landed(m, 12 + 3 * c + j)
                 branch += wide(r2[m, 3 * c + j])
-
-            @pl.when(odd)
-            def _():
-                handed(m, c)
-
             cols = slice(c * 768, (c + 1) * 768)
             out[m, :, cols] = (wide(xin[m, :, cols]) + gate[:, cols] * branch).astype(BF16)
 

time: 302 us -> 302 us (level)
  no operation moved by 1% of the time
where the time goes in v8:
time: 302 us
  Pallas kernels  300 us (99%)
    pallas_call x1, Pallas kernels, per_device(): pl.pallas_call(kernel, out_shape=jax.ShapeDtypeStruct((patches, 16, 3072)...  300 us

profile of v8, /device:TPU:97, one launch (start us, length us, event | category | flops | bytes accessed | tf_op | source)
XLA Modules:
  0.0 301.9 jit_solution(2355185596990318916)
XLA Ops:
  0.0 300.2 %shard_map.136 = bf16[3,16,3072]{2,1,0:T(8,128)(2,1)} custom-call(s32[3]{0:T(128)} %pn.1, s32[3,1,4]{2,1,0:T(1,128)} %bitcast.25, bf16[4,16,3072]{2,1,0:T(8,128)(2,1)} %lat_hbm.1, f32[1,3072]{1,0:T(1,128)} %off_hbm.1, f32[1,3072]{1,0:T(1,128)} %scl_hbm.1, f32[1,3072]{1,0:T(1,128)} %gate_hbm.1, bf16[3,64,128]{2,1,0:T(8,128)(2,1)} %bitcast.24, ...), custom_call_target="tpu_custom_call" | custom-call | flops 10000000000 | bytes 16000000 | tf_op jit(solution)/shard_map/pallas_call | solution.py:568
  300.2 1.7 copy.16
